TPU v7x, 256 devices: a whole 4x4x8 slice. The times are simulated.
256 devices in a mesh: wide: 32 (over y_lo, z, core), narrow: 8 (over x, y_hi).
Axes of the slice: x: 4, y: 4 (y_hi: 2, y_lo: 2; y = y_hi * 2 + y_lo), z: 8, core: 2. Of those that a mesh axis runs over, the one named last changes fastest.
Arguments:
- pair: bfloat16 [768, 768, 128], P('wide', 'narrow'), may hold values from -6 to 6
- tile_mask: int32 [6, 6], replicated, may hold values 0 or 1
- chain_ids: int32 [768], replicated, may hold values from 0 to 3, never falling along the last dimension, each value on 1 to 384 neighbouring positions
- in_gain: float32 [128], replicated, may hold values from 0.1 to 1.9
- in_bias: float32 [128], replicated, may hold values from -3 to 3
- w_ab: bfloat16 [128, 512], replicated, may hold values from -0.5 to 0.5
- w_gate: bfloat16 [128, 128], replicated, may hold values from -0.5 to 0.5
- out_gain: float32 [128], replicated, may hold values from 0.1 to 1.9
- out_bias: float32 [128], replicated, may hold values from -3 to 3
- w_out: bfloat16 [128, 128], replicated, may hold values from -0.5 to 0.5
Outputs:
- update: bfloat16 [768, 768, 128], P('wide', 'narrow')
Inputs may be any that keep to these rules, and one draw needn't show every extreme that they name: `chain_ids`: chain numbers never fall along the tokens.
All inputs are finite; a program needn't handle non-finite values.
Results may differ from a plain program's by a relative error of at most 0.0062.
Values may be sent and summed in bfloat16 or wider, within the bound.
A program may use at most 128 MiB of HBM per device.

v0:
```python
import jax
import jax.numpy as jnp
from jax import lax
from jax.sharding import PartitionSpec as P

TILE = 128


def normalize(values, gain, bias, axis):
    mean = jnp.mean(values, axis=axis, keepdims=True)
    centred = values - mean
    spread = jnp.mean(centred * centred, axis=axis, keepdims=True)
    return centred * lax.rsqrt(spread + 1e-05) * gain + bias


def pair_mask(tile_mask, chain_ids, row_start, rows, cols):
    count = tile_mask.shape[0]
    tiles = jnp.arange(count, dtype=jnp.int32)
    row_index = row_start + jnp.arange(rows, dtype=jnp.int32)
    col_index = jnp.arange(cols, dtype=jnp.int32)
    row_onehot = (row_index[:, None] // TILE == tiles[None, :]).astype(jnp.float32)
    col_onehot = (col_index[:, None] // TILE == tiles[None, :]).astype(jnp.float32)
    blocked = jnp.dot(
        jnp.dot(row_onehot, tile_mask.astype(jnp.float32), precision=lax.Precision.HIGHEST),
        col_onehot.T,
        precision=lax.Precision.HIGHEST,
    )
    row_chain = lax.dynamic_slice_in_dim(chain_ids, row_start, rows)
    same = (row_chain[:, None] == chain_ids[None, :]).astype(jnp.float32)
    return jnp.maximum(blocked, same)


def gated_pair(normed, weights, mask, width):
    proj = jnp.einsum("rkc,cd->drk", normed, weights, preferred_element_type=jnp.float32)
    left_side = mask * jax.nn.sigmoid(proj[:width]) * proj[width : 2 * width]
    right_side = mask * jax.nn.sigmoid(proj[2 * width : 3 * width]) * proj[3 * width :]
    return jnp.stack([left_side, right_side]).astype(jnp.bfloat16)


def shards(pair, tile_mask, chain_ids, in_gain, in_bias, w_ab, w_gate, out_gain, out_bias, w_out):
    rows, cols, width = pair.shape
    hidden = w_out.shape[0]
    slabs = lax.axis_size("narrow")
    slab = hidden // slabs
    total = cols * slabs
    row_start = lax.axis_index("wide") * rows
    normed = normalize(pair.astype(jnp.float32), in_gain, in_bias, 2).astype(jnp.bfloat16)
    gate = jax.nn.sigmoid(
        jnp.einsum("rkc,cd->rkd", normed, w_gate, preferred_element_type=jnp.float32)
    )
    gathered = lax.all_gather(normed, "narrow", axis=1, tiled=True)
    mask = pair_mask(tile_mask, chain_ids, row_start, rows, total)
    grouped = w_ab.reshape(width, 4, hidden)
    own_columns = lax.dynamic_slice_in_dim(
        grouped, lax.axis_index("narrow") * slab, slab, 2
    ).reshape(width, 4 * slab)
    sides = gated_pair(gathered, own_columns, mask, slab)
    left_side = sides[0]
    right_side = sides[1]
    product = jnp.einsum(
        "cik,cjk->cij",
        left_side,
        lax.all_gather(right_side, "wide", axis=1, tiled=True),
        preferred_element_type=jnp.float32,
    ).astype(jnp.bfloat16)
    columns = lax.all_to_all(product, "narrow", split_axis=2, concat_axis=0, tiled=True)
    product_normed = normalize(
        columns.astype(jnp.float32), out_gain[:, None, None], out_bias[:, None, None], 0
    ).astype(jnp.bfloat16)
    projected = jnp.einsum("hrk,hc->rkc", product_normed, w_out, preferred_element_type=jnp.float32)
    return (gate * projected).astype(jnp.bfloat16)


def solution(mesh):
    in_specs = (P("wide", "narrow", None), P(), P(), P(), P(), P(), P(), P(), P(), P())
    out_specs = P("wide", "narrow", None)
    return jax.shard_map(shards, mesh=mesh, in_specs=in_specs, out_specs=out_specs, check_vma=False)
```

profile of v0, /device:TPU:1, one launch (start us, length us, event | category | flops | bytes accessed | tf_op | source)
XLA Modules:
  0.0 273.6 jit_solution(956254252142722408)
XLA Ops:
  6.5 0.0 copy-start
  6.5 0.0 copy-start.1
  6.5 0.0 copy-start.5
  6.5 0.0 copy-start.6
  6.5 0.0 all-gather.3.cloned.1.call-start
  6.6 1.4 convert_reduce_fusion
  8.0 0.0 copy-start.3
  8.0 1.9 fusion.17
  9.9 0.0 copy-start.10
  9.9 0.0 copy-start.9
  10.0 0.0 copy-done.1
  10.0 0.0 copy-done.5
  10.0 0.0 copy-done.6
  10.0 1.5 fusion.20
  11.5 0.0 all-gather.3.cloned.1.call-update
  11.5 0.0 all-gather.5.cloned.1.call-start
  11.6 0.0 copy-done.3
  11.6 0.1 copy.26
  11.7 0.0 copy-done.10
  11.7 0.1 dynamic_slice.6
  11.9 0.0 copy-done.9
  11.9 0.2 fusion.36
  12.1 0.5 convolution_maximum_fusion
  12.5 83.5 %all-gather.3.cloned.1.call-done = bf16[24,768,128]{2,1,0:T(8,128)(2,1)} async-done(((bf16[24,96,128]{2,1,0:T(8,128)(2,1)}), bf16[24,768,128]{2,1,0:T(8,128)(2,1)}) %all-gather.3.cloned.1.call-update) | async-done | bytes 4718608 | tf_op jit(solution)/shard_map/all_gather | solution.py:51
  96.1 4.1 %fusion.42 = f32[64,24,768]{2,0,1:T(8,128)S(1)} fusion(bf16[128,64,1]{0,1,2:T(8,128)(2,1)S(1)} %bitcast.39, bf16[24,768,128]{2,1,0:T(8,128)(2,1)} %all-gather.3.cloned.1.call-done), kind=kOutput, calls=%fused_computation.67 | convolution fusion | flops 301989888 | bytes 9453568 | tf_op jit(solution)/shard_map/rkc,cd->drk/dot_general | solution.py:34
  100.1 1.5 fusion.26
  101.6 0.0 all-gather.5.cloned.1.call-update
  101.6 109.2 %all-gather.5.cloned.1.call-done = bf16[16,768,768]{2,0,1:T(8,128)(2,1)} async-done(((bf16[16,24,768]{2,0,1:T(8,128)(2,1)}), bf16[16,768,768]{2,0,1:T(8,128)(2,1)}) %all-gather.5.cloned.1.call-update) | async-done | bytes 18874384 | tf_op jit(solution)/shard_map/all_gather | solution.py:63
  210.9 17.1 %fusion.14 = bf16[16,24,768]{2,1,0:T(8,128)(2,1)} fusion(bf16[16,768,768]{2,0,1:T(8,128)(2,1)} %all-gather.5.cloned.1.call-done, bf16[16,24,768]{2,0,1:T(8,128)(2,1)S(1)} %get-tuple-element.5), kind=kOutput, calls=%fused_computation.21 | convolution fusion | flops 453279744 | bytes 20054016 | tf_op jit(solution)/shard_map/cik,cjk->cij/dot_general | solution.py:60
  228.0 3.8 %copy.23 = bf16[16,24,768]{1,0,2:T(8,128)(2,1)S(1)} copy(bf16[16,24,768]{2,1,0:T(8,128)(2,1)} %fusion.14) | data formatting | bytes 1179648 | tf_op jit(solution)/shard_map/convert_element_type | solution.py:65
  231.9 4.6 %reshape.127 = bf16[8,2,18432]{2,1,0:T(2,128)(2,1)} reshape(bf16[768,16,24]{2,1,0:T(8,128)(2,1)S(1)} %bitcast.36) | data formatting | bytes 1179648
  236.5 0.0 copy-start.2
  236.5 6.6 %all-to-all-start = ((bf16[8,2,18432]{2,1,0:T(2,128)(2,1)}), bf16[8,2,18432]{2,1,0:T(2,128)(2,1)S(1)}, u32[]{:S(2)}, u32[]{:S(2)}) async-start(bf16[8,2,18432]{2,1,0:T(2,128)(2,1)} %reshape.127), calls=%async_computation | async-start | bytes 1179648 | tf_op jit(solution)/shard_map/all_to_all | solution.py:66
  243.0 0.0 copy-done
  243.0 0.0 copy-done.2
  243.0 0.5 fusion.12
  243.5 10.7 %all-to-all-done = bf16[8,2,18432]{2,1,0:T(2,128)(2,1)S(1)} async-done(((bf16[8,2,18432]{2,1,0:T(2,128)(2,1)}), bf16[8,2,18432]{2,1,0:T(2,128)(2,1)S(1)}, u32[]{:S(2)}, u32[]{:S(2)}) %all-to-all-start) | async-done | bytes 589856 | tf_op jit(solution)/shard_map/all_to_all | solution.py:66
  254.2 5.3 %reshape.128 = bf16[768,16,24]{2,1,0:T(8,128)(2,1)} reshape(bf16[8,2,18432]{2,1,0:T(2,128)(2,1)S(1)} %all-to-all-done) | data formatting | bytes 1179648
  259.5 4.5 %copy.24 = f32[16,24,8,96]{3,1,0,2:T(8,128)S(1)} copy(bf16[16,24,8,96]{1,0,3,2:T(8,128)(2,1)} %bitcast.37) | data formatting | bytes 1769472 | tf_op jit(solution)/shard_map/convert_element_type | solution.py:68
  264.0 0.2 bitcast_reduce_fusion
  264.2 0.0 copy-start.7
  264.2 0.0 copy-start.8
  264.2 0.3 fusion.7
  264.5 0.3 copy-done.7
  264.8 0.0 copy-done.8
  264.8 0.0 copy-start.4
  264.8 0.3 fusion.5
  265.2 0.4 copy-done.4
  265.6 1.2 fusion.13
  (7 shorter events, 0.1 us)
Async XLA Ops:
  6.5 236.5 %copy-start = (bf16[128,128]{1,0:T(8,128)(2,1)S(1)}, bf16[128,128]{1,0:T(8,128)(2,1)}, u32[]{:S(2)}) copy-start(bf16[128,128]{1,0:T(8,128)(2,1)} %param.16) | copy-start | bytes 98308
  6.5 3.4 %copy-start.1 = (bf16[24,96,128]{2,1,0:T(8,128)(2,1)S(1)}, bf16[24,96,128]{2,1,0:T(8,128)(2,1)}, u32[]{:S(2)}) copy-start(bf16[24,96,128]{2,1,0:T(8,128)(2,1)} %param.10) | copy-start | bytes 1769476
  6.5 3.4 %copy-start.5 = (f32[128]{0:T(128)S(1)}, f32[128]{0:T(128)}, u32[]{:S(2)}) copy-start(f32[128]{0:T(128)} %param.14) | copy-start | bytes 1540
  6.5 3.4 %copy-start.6 = (f32[128]{0:T(128)S(1)}, f32[128]{0:T(128)}, u32[]{:S(2)}) copy-start(f32[128]{0:T(128)} %param.13) | copy-start | bytes 1540
  6.5 89.5 %all-gather.3.cloned.1.call-start = ((), (), s32[]{:S(2)}) async-start(), calls=%async_computation.1 | async-start | bytes 5308416 | tf_op jit(solution)/shard_map/all_gather | solution.py:51
  8.0 3.6 %copy-start.3 = (bf16[128,512]{1,0:T(8,128)(2,1)S(1)}, bf16[128,512]{1,0:T(8,128)(2,1)}, u32[]{:S(2)}) copy-start(bf16[128,512]{1,0:T(8,128)(2,1)} %param.15) | copy-start | bytes 393220
  9.9 1.8 copy-start.10
  9.9 1.9 copy-start.9
  11.5 199.3 %all-gather.5.cloned.1.call-start = ((), (), s32[]{:S(2)}) async-start(), calls=%async_computation.2 | async-start | bytes 19464192 | tf_op jit(solution)/shard_map/all_gather | solution.py:63
  236.5 6.6 %copy-start.2 = (bf16[24,96,128]{2,1,0:T(8,128)(2,1)S(1)}, bf16[24,96,128]{2,1,0:T(8,128)(2,1)}, u32[]{:S(2)}) copy-start(bf16[24,96,128]{2,1,0:T(8,128)(2,1)} %fusion.20) | copy-start | bytes 1769476
  236.5 17.7 %all-to-all-start = ((bf16[8,2,18432]{2,1,0:T(2,128)(2,1)}), bf16[8,2,18432]{2,1,0:T(2,128)(2,1)S(1)}, u32[]{:S(2)}, u32[]{:S(2)}) async-start(bf16[8,2,18432]{2,1,0:T(2,128)(2,1)} %reshape.127), calls=%async_computation | async-start | bytes 1179648 | tf_op jit(solution)/shard_map/all_to_all | solution.py:66
  264.2 0.7 copy-start.7
  264.2 0.7 copy-start.8
  264.8 0.8 copy-start.4
Sparse Core Ops, SparseCore 0:
  11.7 84.3 all-gather.2
  101.8 109.0 all-gather.4
where the time goes:
time: 274 us
  waiting for transfers between devices  204 us (74%)
  matrix products  23.5 us (9%)
  local copies, waits for them, and re-layouts  19.2 us (7%)
  between operations  13.6 us (5%)
  other arithmetic  7.11 us (3%)
  starting transfers between devices  6.63 us (2%)
    all_gather x1, waiting for transfers between devices, shards(): lax.all_gather(right_side, 'wide', axis=1, tiled=True)  109 us
    all_gather x1, waiting for transfers between devices, shards(): gathered = lax.all_gather(normed, 'narrow', axis=1, tiled=True)  83.5 us
    dot_general x1, matrix products, shards(): jnp.einsum('cik,cjk->cij', left_side, lax.all_gather(right_side, 'wide',...  17.1 us
    unnamed x24, local copies, waits for them, and re-layouts  10.7 us
    all_to_all x1, waiting for transfers between devices, shards(): lax.all_to_all(product, 'narrow', split_axis=2, concat_axis=0, tiled=True)  10.7 us
    all_to_all x1, starting transfers between devices, shards(): lax.all_to_all(product, 'narrow', split_axis=2, concat_axis=0, tiled=True)  6.56 us
  transfers between devices with their start and end apart: 3, of which 3 were waited for; matrix products, arithmetic and copies ran while one was open for 0% of the time, Pallas kernels for 0%

commit v1 on v0

v1 whole, which is shorter than its diff:
```python
import functools

import jax
import jax.numpy as jnp
from jax import lax
from jax.experimental import pallas as pl
from jax.experimental.pallas import tpu as pltpu
from jax.sharding import PartitionSpec as P

MESH = pl.DeviceIdType.MESH
F32, BF16 = jnp.float32, jnp.bfloat16
CHIPS = 128
ROWS, COLS, C = 24, 96, 128
MSG = 40
TILES = 24
EPS = 1e-05


def sigmoid(x):
    return 0.5 * jnp.tanh(0.5 * x) + 0.5


def dot(a, b, ca, cb):
    return lax.dot_general(a, b, (((ca,), (cb,)), ((), ())), preferred_element_type=F32)


def keep_mask(wide, narrow, tile_ref, chain_ref):
    tile = lax.broadcasted_iota(jnp.int32, (TILES, 128), 0)
    lane = lax.broadcasted_iota(jnp.int32, (TILES, 128), 1)
    body, main = tile < 16, lane < 96
    i = jnp.where(body & jnp.logical_not(main), 16 + tile % 8, tile)
    k = jnp.where(body, jnp.where(main, lane, lane - 96 + 32 * (tile // 8)), 64 + lane % 32)
    i = i + wide * ROWS
    k = k + narrow * COLS
    chain_i = jnp.zeros((TILES, 128), jnp.int32)
    chain_k = jnp.zeros((TILES, 128), jnp.int32)
    chains = chain_ref[...]
    for q in range(1, 4):
        below = (chains < q).astype(F32)
        start = jnp.sum(jnp.sum(below, axis=0, keepdims=True), axis=1, keepdims=True).astype(jnp.int32)
        chain_i = chain_i + (i >= start).astype(jnp.int32)
        chain_k = chain_k + (k >= start).astype(jnp.int32)
    same = (chain_i == chain_k).astype(F32)
    row_tile, col_tile = i // 128, k // 128
    blocked = jnp.zeros((TILES, 128), F32)
    for a in range(6):
        in_row = row_tile == a
        for b in range(6):
            value = tile_ref[a, b].astype(F32)
            blocked = blocked + jnp.where(in_row & (col_tile == b), value, 0.0)
    return jnp.maximum(blocked, same)


def kernel(
    pair_ref, tile_ref, chain_ref, in_gain_ref, in_bias_ref, w_ab_ref, w_gate_ref, out_gain_ref, out_bias_ref, w_out_ref,
    out_ref,
    normed_ref, packed_ref, mask_ref, w_t_ref, stage_ref, send_ref, recv_ref, gate_ref, a_ref, b_ref, back_ref, home_ref,
    sums_ref, s_send, s_recv, s_swap_send, s_swap_recv, s_back, s_home,
):
    wide, narrow = lax.axis_index("wide"), lax.axis_index("narrow")
    w16, core = wide // 2, wide % 2
    y_lo, z = wide // 16, (wide // 2) % 8
    x, y = narrow // 2, (narrow % 2) * 2 + y_lo
    me = w16 * 8 + narrow

    def peer(d):
        pz = (z + d % 8) % 8
        py = (y + (d // 8) % 4) % 4
        px = (x + d // 32) % 4
        p16 = (py % 2) * 8 + pz
        pn = px * 2 + py // 2
        return p16 * 8 + pn, (p16 * 2 + core, pn)

    sibling = (w16 * 2 + 1 - core, narrow)
    barrier = pltpu.get_barrier_semaphore()
    pl.semaphore_signal(barrier, inc=1, device_id=sibling, device_id_type=MESH)

    def greet(d, _):
        pl.semaphore_signal(barrier, inc=1, device_id=peer(d)[1], device_id_type=MESH)
        return 0

    lax.fori_loop(1, CHIPS, greet, 0)

    w_t_ref[...] = w_ab_ref[...].T
    mask_ref[...] = keep_mask(wide, narrow, tile_ref, chain_ref)

    def norm_row(i):
        values = pair_ref[i].astype(F32)
        mean = jnp.mean(values, axis=1, keepdims=True)
        centred = values - mean
        spread = jnp.mean(centred * centred, axis=1, keepdims=True)
        normed = (centred * lax.rsqrt(spread + EPS) * in_gain_ref[...] + in_bias_ref[...]).astype(BF16)
        normed_ref[i] = normed
        return normed

    def norm_body(i, _):
        packed_ref[i, 0:96] = norm_row(i)
        return 0

    def norm_tail(r, _):
        normed = norm_row(16 + r)
        packed_ref[r, 96:128] = normed[0:32]
        packed_ref[8 + r, 96:128] = normed[32:64]
        last = normed[64:96]
        for q in range(4):
            packed_ref[16 + r, 32 * q : 32 * q + 32] = last
        return 0

    lax.fori_loop(0, 16, norm_body, 0)
    lax.fori_loop(0, 8, norm_tail, 0)

    def sides(t):
        proj = dot(w_t_ref[...], packed_ref[t], 1, 1)
        mask = mask_ref[pl.ds(t, 1), :]
        left = mask * sigmoid(proj[0:128]) * proj[128:256]
        right = mask * sigmoid(proj[256:384]) * proj[384:512]
        return left, right

    def project(t, _):
        left, right = sides(t)
        stage_ref[pl.ds(t, CHIPS, stride=MSG), :] = left
        stage_ref[pl.ds(16 + t, CHIPS, stride=MSG), :] = right
        return 0

    lane8 = lax.broadcasted_iota(jnp.int32, (8, 128), 1)

    def project_tail(t, _):
        left, right = sides(t)
        lane = lax.broadcasted_iota(jnp.int32, (128, 128), 1)
        stage_ref[pl.ds(16 + t, CHIPS, stride=MSG), :] = jnp.where(lane < 32, left, right)
        return 0

    lax.fori_loop(0, 16, project, 0)
    lax.fori_loop(16, 24, project_tail, 0)

    def cast(c, _):
        start = pl.multiple_of(c * MSG, 8)
        send_ref[c] = stage_ref[pl.ds(start, MSG), :].astype(BF16)
        return 0

    lax.fori_loop(0, CHIPS, cast, 0, unroll=4)

    pl.semaphore_wait(barrier, CHIPS)

    def send(d, _):
        chip, device = peer(d)
        pltpu.make_async_remote_copy(
            src_ref=send_ref.at[chip], dst_ref=recv_ref.at[me], send_sem=s_send, recv_sem=s_recv,
            device_id=device, device_id_type=MESH,
        ).start()
        return 0

    lax.fori_loop(1, CHIPS, send, 0)
    recv_ref[me] = send_ref[me]

    def gates(i, _):
        gate_ref[i] = sigmoid(dot(normed_ref[i], w_gate_ref[...], 1, 0))
        return 0

    lax.fori_loop(0, ROWS, gates, 0)
    for p in range(8):
        b_ref[p, 96:128] = jnp.zeros((32, 1024), BF16)

    others = pl.ds(0, CHIPS - 1)
    pltpu.make_async_copy(recv_ref.at[others], recv_ref.at[others], s_recv).wait()
    pltpu.make_async_copy(send_ref.at[others], send_ref.at[others], s_send).wait()

    def unpack(slot):
        f = recv_ref[slot].astype(F32)
        lane = lane8
        low = f[32:40]
        zero = jnp.zeros((8, 128), F32)

        def rest(top, middle, shift):
            return jnp.where(
                lane < 32, pltpu.roll(top, 32, 1),
                jnp.where(lane < 64, pltpu.roll(middle, 64, 1), jnp.where(lane < 96, pltpu.roll(low, shift, 1), zero)),
            )

        left = [jnp.where(lane < 96, f[0:8], zero), jnp.where(lane < 96, f[8:16], zero), rest(f[0:8], f[8:16], 64)]
        right = [f[16:24], f[24:32], rest(f[16:24], f[24:32], 32)]
        return left, right

    def assemble(p, _):
        for n in range(8):
            left0, right0 = unpack(p * 16 + n)
            left1, right1 = unpack(p * 16 + 8 + n)
            columns = slice(128 * n, 128 * n + 128)
            a_ref[pl.ds(pl.multiple_of(p * 48, 16), 48), columns] = jnp.concatenate(left0 + left1, axis=0).astype(BF16)
            b_ref[p, pl.ds(pl.multiple_of(core * 48, 16), 48), columns] = jnp.concatenate(right0 + right1, axis=0).astype(BF16)
        return 0

    lax.fori_loop(0, 8, assemble, 0)

    half = b_ref.at[:, pl.ds(pl.multiple_of(core * 48, 16), 48), :]
    swap = pltpu.make_async_remote_copy(
        src_ref=half, dst_ref=half, send_sem=s_swap_send, recv_sem=s_swap_recv, device_id=sibling, device_id_type=MESH
    )
    swap.start()
    swap.wait()

    def multiply(p, _):
        product = dot(a_ref[...], b_ref[p], 1, 1)
        for w in range(16):
            back_ref[w * 8 + p] = product[24 * w : 24 * w + 24].astype(BF16)
        return 0

    lax.fori_loop(0, 8, multiply, 0)

    def send_back(d, _):
        chip, device = peer(d)
        pltpu.make_async_remote_copy(
            src_ref=back_ref.at[chip], dst_ref=home_ref.at[me], send_sem=s_back, recv_sem=s_home,
            device_id=device, device_id_type=MESH,
        ).start()
        return 0

    lax.fori_loop(1, CHIPS, send_back, 0)
    home_ref[me] = back_ref[me]
    pltpu.make_async_copy(home_ref.at[others], home_ref.at[others], s_home).wait()
    pltpu.make_async_copy(back_ref.at[others], back_ref.at[others], s_back).wait()

    def widen(c, _):
        sums_ref[pl.ds(pl.multiple_of(c * ROWS, 8), ROWS), :] = home_ref[c].astype(F32)
        return 0

    lax.fori_loop(0, CHIPS, widen, 0, unroll=4)

    def finish(i, _):
        values = sums_ref[pl.ds(i, CHIPS, stride=ROWS), :]
        mean = jnp.mean(values, axis=0, keepdims=True)
        centred = values - mean
        spread = jnp.mean(centred * centred, axis=0, keepdims=True)
        normed = (centred * lax.rsqrt(spread + EPS) * out_gain_ref[...] + out_bias_ref[...]).astype(BF16)
        projected = dot(normed, w_out_ref[...], 0, 0)
        natural = jnp.concatenate([projected[0:24], projected[48:72], projected[24:48], projected[72:96]], axis=0)
        out_ref[i] = (gate_ref[i] * natural).astype(BF16)
        return 0

    lax.fori_loop(0, ROWS, finish, 0)


def shards(pair, tile_mask, chain_ids, in_gain, in_bias, w_ab, w_gate, out_gain, out_bias, w_out):
    vmem = pl.BlockSpec(memory_space=pltpu.VMEM)
    smem = pl.BlockSpec(memory_space=pltpu.SMEM)
    return pl.pallas_call(
        kernel,
        out_shape=jax.ShapeDtypeStruct((ROWS, COLS, C), BF16),
        in_specs=[vmem, smem] + [vmem] * 8,
        out_specs=vmem,
        scratch_shapes=[
            pltpu.VMEM((ROWS, COLS, C), BF16),
            pltpu.VMEM((TILES, 128, C), BF16),
            pltpu.VMEM((TILES, 128), F32),
            pltpu.VMEM((512, C), BF16),
            pltpu.VMEM((CHIPS * MSG, 128), F32),
            pltpu.VMEM((CHIPS, MSG, 128), BF16),
            pltpu.VMEM((CHIPS, MSG, 128), BF16),
            pltpu.VMEM((ROWS, COLS, C), F32),
            pltpu.VMEM((384, 1024), BF16),
            pltpu.VMEM((8, 128, 1024), BF16),
            pltpu.VMEM((CHIPS, ROWS, 128), BF16),
            pltpu.VMEM((CHIPS, ROWS, 128), BF16),
            pltpu.VMEM((CHIPS * ROWS, 128), F32),
        ]
        + [pltpu.SemaphoreType.DMA(())] * 6,
        compiler_params=pltpu.CompilerParams(collective_id=1, has_side_effects=True, vmem_limit_bytes=48 << 20),
    )(
        pair, tile_mask, chain_ids.reshape(6, 128), in_gain.reshape(1, C), in_bias.reshape(1, C), w_ab, w_gate,
        jnp.broadcast_to(out_gain[:, None], (C, 128)), jnp.broadcast_to(out_bias[:, None], (C, 128)), w_out,
    )


def solution(mesh):
    in_specs = (P("wide", "narrow", None), P(), P(), P(), P(), P(), P(), P(), P(), P())
    out_specs = P("wide", "narrow", None)
    return jax.shard_map(shards, mesh=mesh, in_specs=in_specs, out_specs=out_specs, check_vma=False)
```

time: 274 us -> 93.1 us (0.34)
  waiting for transfers between devices: 204 us -> 0 us
  Pallas kernels: 0 us -> 87.1 us
  matrix products: 23.5 us -> 0 us
  local copies, waits for them, and re-layouts: 19.2 us -> 5.61 us
  between operations: 13.6 us -> 0.08 us
  other arithmetic: 7.11 us -> 0 us
  starting transfers between devices: 6.63 us -> 0 us
    all_gather x2 -> x0, waiting for transfers between devices: 193 us -> none  [the longest x1 109 us: shards(): lax.all_gather(right_side, 'wide', axis=1, tiled=True)]
    pallas_call x0 -> x1, Pallas kernels: none -> 87.1 us  [shards(): pl.pallas_call(kernel, out_shape=jax.ShapeDtypeStruct((ROWS, COLS, C), BF...]
    dot_general x6 -> x0, matrix products: 23.5 us -> none  [the longest x1 17.1 us: shards(): jnp.einsum('cik,cjk->cij', left_side, lax.all_gather(right_side, 'wide',...]
    all_to_all x1 -> x0, waiting for transfers between devices: 10.7 us -> none  [shards(): lax.all_to_all(product, 'narrow', split_axis=2, concat_axis=0, tiled=True)]
    convert_element_type x2 -> x0, local copies, waits for them, and re-layouts: 8.33 us -> none  [the longest x1 4.52 us: shards(): columns.astype(jnp.float32)]
    unnamed x24 -> x17, local copies, waits for them, and re-layouts: 10.7 us -> 4.1 us
    all_to_all x1 -> x0, starting transfers between devices: 6.56 us -> none  [shards(): lax.all_to_all(product, 'narrow', split_axis=2, concat_axis=0, tiled=True)]
    reduce_sum x4 -> x0, other arithmetic: 3.73 us -> none  [the longest x2 2.17 us: normalize(): spread = jnp.mean(centred * centred, axis=axis, keepdims=True)]
  transfers between devices with their start and end apart: 3 -> 0, of which waited for: 3 -> 0; matrix products, arithmetic and copies ran while one was open for 0% -> 0% of each run, Pallas kernels for 0% -> 0%
where the time goes in v1:
time: 93.1 us; the launch traced here: 92.7 us
  Pallas kernels  87.1 us (94%)
  local copies, waits for them, and re-layouts  5.61 us (6%)
    pallas_call x1, Pallas kernels, shards(): pl.pallas_call(kernel, out_shape=jax.ShapeDtypeStruct((ROWS, COLS, C), BF...  87.1 us
    unnamed x17, local copies, waits for them, and re-layouts  4.1 us

profile of v1, /device:TPU:1, one launch (start us, length us, event | category | flops | bytes accessed | tf_op | source)
XLA Modules:
  0.0 92.7 jit_solution(11364903414859804590)
XLA Ops:
  0.0 0.0 copy-start.1
  0.0 0.8 broadcast_in_dim.4.out_gain_ref
  0.8 0.0 copy-start.4
  0.8 0.0 copy-start.6
  0.8 0.0 copy-start.7
  0.8 0.8 broadcast_in_dim.5.out_bias_ref
  1.6 0.0 copy-done.1
  1.6 0.0 copy-done.4
  1.6 0.0 copy-done.6
  1.6 0.0 copy-done.7
  1.6 0.0 copy-start
  1.6 1.1 %copy-done = bf16[24,96,128]{2,1,0:T(8,128)(2,1)S(1)} copy-done((bf16[24,96,128]{2,1,0:T(8,128)(2,1)S(1)}, bf16[24,96,128]{2,1,0:T(8,128)(2,1)}, u32[]{:S(2)}) %copy-start) | copy-done | bytes 589848
  2.7 0.0 copy-start.2
  2.7 0.8 copy-done.2
  3.4 0.0 copy-start.3
  3.4 0.8 copy-done.3
  4.2 0.0 copy-start.5
  4.2 0.7 copy-done.5
  4.9 87.1 %shard_map.100 = bf16[24,96,128]{2,1,0:T(8,128)(2,1)S(1)} custom-call(bf16[24,96,128]{2,1,0:T(8,128)(2,1)S(1)} %copy-done, s32[6,6]{1,0:T(8,128)S(1)} %copy-done.4, s32[6,128]{1,0:T(8,128)S(1)} %bitcast.3, f32[1,128]{1,0:T(1,128)S(1)} %bitcast.4, f32[1,128]{1,0:T(1,128)S(1)} %bitcast.5, bf16[128,512]{1,0:T(8,128)(2,1)S(1)} %copy-done.1, ...), custom_call_target="tpu_custom_call" | custom-call | tf_op jit(solution)/shard_map/pallas_call | solution.py:246
  91.9 0.8 copy.12
Async XLA Ops:
  0.0 1.6 %copy-start.1 = (bf16[128,512]{1,0:T(8,128)(2,1)S(1)}, bf16[128,512]{1,0:T(8,128)(2,1)}, u32[]{:S(2)}) copy-start(bf16[128,512]{1,0:T(8,128)(2,1)} %w_ab_ref.1) | copy-start | bytes 393220
  0.8 0.8 copy-start.4
  0.8 0.8 copy-start.6
  0.8 0.8 copy-start.7
  1.6 1.1 %copy-start = (bf16[24,96,128]{2,1,0:T(8,128)(2,1)S(1)}, bf16[24,96,128]{2,1,0:T(8,128)(2,1)}, u32[]{:S(2)}) copy-start(bf16[24,96,128]{2,1,0:T(8,128)(2,1)} %pair_ref.1) | copy-start | bytes 1769476
  2.7 0.8 copy-start.2
  3.4 0.8 copy-start.3
  4.2 0.7 copy-start.5

commit v2 on v1

v2 whole, which is shorter than its diff:
```python
import functools

import jax
import jax.numpy as jnp
from jax import lax
from jax.experimental import pallas as pl
from jax.experimental.pallas import tpu as pltpu
from jax.sharding import PartitionSpec as P

MESH = pl.DeviceIdType.MESH
F32, BF16 = jnp.float32, jnp.bfloat16
CHIPS = 128
ROWS, COLS, C = 24, 96, 128
MSG = 40
TILES = 24
EPS = 1e-05


def sigmoid(x):
    return 0.5 * jnp.tanh(0.5 * x) + 0.5


def dot(a, b, ca, cb):
    return lax.dot_general(a, b, (((ca,), (cb,)), ((), ())), preferred_element_type=F32)


def keep_mask(wide, narrow, tile_ref, chain_ref):
    tile = lax.broadcasted_iota(jnp.int32, (TILES, 128), 0)
    lane = lax.broadcasted_iota(jnp.int32, (TILES, 128), 1)
    body, main = tile < 16, lane < 96
    i = jnp.where(body & jnp.logical_not(main), 16 + tile % 8, tile)
    k = jnp.where(body, jnp.where(main, lane, lane - 96 + 32 * (tile // 8)), 64 + lane % 32)
    i = i + wide * ROWS
    k = k + narrow * COLS
    chain_i = jnp.zeros((TILES, 128), jnp.int32)
    chain_k = jnp.zeros((TILES, 128), jnp.int32)
    chains = chain_ref[...]
    for q in range(1, 4):
        below = (chains < q).astype(F32)
        start = jnp.sum(jnp.sum(below, axis=0, keepdims=True), axis=1, keepdims=True).astype(jnp.int32)
        chain_i = chain_i + (i >= start).astype(jnp.int32)
        chain_k = chain_k + (k >= start).astype(jnp.int32)
    same = (chain_i == chain_k).astype(F32)
    row_tile, col_tile = i // 128, k // 128
    blocked = jnp.zeros((TILES, 128), F32)
    for a in range(6):
        in_row = row_tile == a
        for b in range(6):
            value = tile_ref[a : a + 1, b : b + 1].astype(F32)
            blocked = blocked + jnp.where(in_row & (col_tile == b), value, 0.0)
    return jnp.maximum(blocked, same)


def kernel(
    pair_hbm, tile_hbm, chain_hbm, in_gain_hbm, in_bias_hbm, w_ab_hbm, w_gate_hbm, out_gain_hbm, out_bias_hbm, w_out_hbm,
    out_ref,
    pair_ref, tile_ref, chain_ref, in_gain_ref, in_bias_ref, w_ab_ref, w_gate_ref, out_gain_ref, out_bias_ref, w_out_ref,
    normed_ref, packed_ref, mask_ref, w_t_ref, stage_ref, send_ref, recv_ref, gate_ref, a_ref, b_ref, total_ref, back_ref,
    home_ref, sums_ref, gain_ref, bias_ref,
    s_in, s_line, s_plane, s_send, s_recv, s_swap_send, s_swap_recv, s_back, s_home,
):
    wide, narrow = lax.axis_index("wide"), lax.axis_index("narrow")
    w16, core = wide // 2, wide % 2
    y_lo, z = wide // 16, w16 % 8
    x, y = narrow // 2, (narrow % 2) * 2 + y_lo
    me = x * 32 + y * 8 + z

    def device_at(px, py, pz):
        return ((py % 2) * 16 + pz * 2 + core, px * 2 + py // 2)

    sibling = (w16 * 2 + 1 - core, narrow)
    line_z = [device_at(x, y, (z + d) % 8) for d in range(1, 8)]
    line_y = [device_at(x, (y + d) % 4, z) for d in range(1, 4)]
    line_x = [device_at((x + d) % 4, y, z) for d in range(1, 4)]

    inputs = [
        pltpu.make_async_copy(source, target, s_in.at[at])
        for at, (source, target) in enumerate((
            (pair_hbm, pair_ref), (tile_hbm, tile_ref), (chain_hbm, chain_ref), (in_gain_hbm, in_gain_ref),
            (in_bias_hbm, in_bias_ref), (w_ab_hbm, w_ab_ref), (w_gate_hbm, w_gate_ref), (out_gain_hbm, out_gain_ref),
            (out_bias_hbm, out_bias_ref), (w_out_hbm, w_out_ref),
        ))
    ]
    for copy in inputs:
        copy.start()

    barrier = pltpu.get_barrier_semaphore()
    greeted = [sibling] + line_z + line_y + line_x
    for device in greeted:
        pl.semaphore_signal(barrier, inc=1, device_id=device, device_id_type=MESH)

    for copy in inputs:
        copy.wait()

    w_t_ref[...] = w_ab_ref[...].T
    mask_ref[...] = keep_mask(wide, narrow, tile_ref, chain_ref)
    gain_ref[...] = jnp.broadcast_to(out_gain_ref[...], (C, 128)).T
    bias_ref[...] = jnp.broadcast_to(out_bias_ref[...], (C, 128)).T

    pl.semaphore_wait(barrier, len(greeted))
    for device in line_y:
        pl.semaphore_signal(s_line, inc=1, device_id=device, device_id_type=MESH)

    def norm_row(i):
        values = pair_ref[i].astype(F32)
        mean = jnp.mean(values, axis=1, keepdims=True)
        centred = values - mean
        spread = jnp.mean(centred * centred, axis=1, keepdims=True)
        normed = (centred * lax.rsqrt(spread + EPS) * in_gain_ref[...] + in_bias_ref[...]).astype(BF16)
        normed_ref[i] = normed
        return normed

    def norm_body(i, _):
        packed_ref[i, 0:96] = norm_row(i)
        return 0

    def norm_tail(r, _):
        normed = norm_row(16 + r)
        packed_ref[r, 96:128] = normed[0:32]
        packed_ref[8 + r, 96:128] = normed[32:64]
        last = normed[64:96]
        for q in range(4):
            packed_ref[16 + r, 32 * q : 32 * q + 32] = last
        return 0

    lax.fori_loop(0, 16, norm_body, 0, unroll=2)
    lax.fori_loop(0, 8, norm_tail, 0, unroll=2)

    pl.semaphore_wait(s_line, len(line_y))
    for device in line_x:
        pl.semaphore_signal(s_plane, inc=1, device_id=device, device_id_type=MESH)

    lane32 = lax.broadcasted_iota(jnp.int32, (32, 128), 1)

    def send_chunk(dx):
        px = (x + dx) % 4
        first = pl.multiple_of(px * 32, 32)
        weights = jnp.concatenate([w_t_ref[pl.ds(g * 128 + first, 32), :] for g in range(4)], axis=0)

        def sides(t):
            proj = dot(weights, packed_ref[pl.ds(t, 2)].reshape(256, C), 1, 1)
            result = []
            for q in range(2):
                part = proj[:, 128 * q : 128 * q + 128]
                mask = mask_ref[pl.ds(t + q, 1), :]
                left = mask * sigmoid(part[0:32]) * part[32:64]
                right = mask * sigmoid(part[64:96]) * part[96:128]
                result.append((left, right))
            return result

        def project(h, _):
            t = 2 * h
            for q, (left, right) in enumerate(sides(t)):
                stage_ref[pl.ds(t + q, 32, stride=MSG), :] = left
                stage_ref[pl.ds(16 + t + q, 32, stride=MSG), :] = right
            return 0

        def project_tail(h, _):
            t = 2 * h
            for q, (left, right) in enumerate(sides(t)):
                stage_ref[pl.ds(16 + t + q, 32, stride=MSG), :] = jnp.where(lane32 < 32, left, right)
            return 0

        lax.fori_loop(0, 8, project, 0, unroll=2)
        lax.fori_loop(8, 12, project_tail, 0, unroll=2)

        def cast(c):
            start = pl.multiple_of(c * MSG, 8)
            send_ref[px * 32 + c] = stage_ref[pl.ds(start, MSG), :].astype(BF16)

        def send(d, _):
            py, pz = (y + d // 8) % 4, (z + d % 8) % 8
            slot = px * 32 + py * 8 + pz
            pltpu.make_async_remote_copy(
                src_ref=send_ref.at[slot], dst_ref=recv_ref.at[me], send_sem=s_send, recv_sem=s_recv.at[dx],
                device_id=device_at(px, py, pz), device_id_type=MESH,
            ).start()
            return 0

        def cast_body(c, _):
            cast(c)
            return 0

        lax.fori_loop(0, 32, cast_body, 0, unroll=4)
        if dx == 0:
            pl.semaphore_wait(s_plane, len(line_x))
        lax.fori_loop(1 if dx == 0 else 0, 32, send, 0)
        if dx == 0:
            recv_ref[me] = send_ref[me]

    for dx in range(4):
        send_chunk(dx)

    def gates(i, _):
        gate_ref[i] = sigmoid(dot(normed_ref[i], w_gate_ref[...], 1, 0))
        return 0

    lax.fori_loop(0, ROWS, gates, 0)
    for dx in range(4):
        for p in range(8):
            b_ref[dx, p, 96:128] = jnp.zeros((32, 256), BF16)

    lane = lax.broadcasted_iota(jnp.int32, (8, 128), 1)

    def unpack(slot):
        f = recv_ref[slot].astype(F32)
        low = f[32:40]
        zero = jnp.zeros((8, 128), F32)

        def rest(top, middle, shift):
            return jnp.where(
                lane < 32, pltpu.roll(top, 32, 1),
                jnp.where(lane < 64, pltpu.roll(middle, 64, 1), jnp.where(lane < 96, pltpu.roll(low, shift, 1), zero)),
            )

        left = [jnp.where(lane < 96, f[0:8], zero), jnp.where(lane < 96, f[8:16], zero), rest(f[0:8], f[8:16], 64)]
        right = [f[16:24], f[24:32], rest(f[16:24], f[24:32], 32)]
        return left, right

    mine = pl.ds(pl.multiple_of(core * 48, 16), 48)

    def swap(dx):
        half = b_ref.at[dx, :, mine, :]
        return pltpu.make_async_remote_copy(
            src_ref=half, dst_ref=half, send_sem=s_swap_send.at[dx], recv_sem=s_swap_recv.at[dx], device_id=sibling,
            device_id_type=MESH,
        )

    def receive(dx):
        arrived = recv_ref.at[pl.ds(0, 31 if dx == 0 else 32)]
        pltpu.make_async_copy(arrived, arrived, s_recv.at[dx]).wait()
        first = ((x + 4 - dx) % 4) * 32

        def assemble(p, _):
            for q in range(2):
                left0, right0 = unpack(first + 16 * q + 2 * p)
                left1, right1 = unpack(first + 16 * q + 2 * p + 1)
                columns = slice(128 * q, 128 * q + 128)
                rows = pl.ds(pl.multiple_of(p * 48, 16), 48)
                a_ref[dx, rows, columns] = jnp.concatenate(left0 + left1, axis=0).astype(BF16)
                b_ref[dx, p, mine, columns] = jnp.concatenate(right0 + right1, axis=0).astype(BF16)
            return 0

        lax.fori_loop(0, 8, assemble, 0)
        swap(dx).start()

    def partial(dx, px):
        return dot(a_ref[dx], b_ref[dx, pl.ds(2 * px, 2)].reshape(256, 256), 1, 1)

    def multiply(dx):
        swap(dx).wait()

        def step(px, _):
            if dx == 0:
                total_ref[px] = partial(dx, px)
            else:
                total_ref[px] += partial(dx, px)
            return 0

        lax.fori_loop(0, 4, step, 0)

    for dx in range(4):
        receive(dx)
        if dx > 0:
            multiply(dx - 1)
    swap(3).wait()

    def back(q, _):
        px = (x + q) % 4
        product = (total_ref[px] + partial(3, px)).astype(BF16)
        for h in range(2):
            for w in range(16):
                back_ref[px * 32 + h * 16 + w] = product[24 * w : 24 * w + 24, 128 * h : 128 * h + 128]

        def send(d, _):
            py, pz = (y + d // 8) % 4, (z + d % 8) % 8
            pltpu.make_async_remote_copy(
                src_ref=back_ref.at[px * 32 + py * 8 + pz], dst_ref=home_ref.at[me], send_sem=s_back, recv_sem=s_home,
                device_id=device_at(px, py, pz), device_id_type=MESH,
            ).start()
            return 0

        lax.fori_loop(jnp.where(q == 0, 1, 0), 32, send, 0)
        return 0

    lax.fori_loop(0, 4, back, 0)
    home_ref[me] = back_ref[me]
    others = pl.ds(0, CHIPS - 1)
    pltpu.make_async_copy(send_ref.at[others], send_ref.at[others], s_send).wait()
    pltpu.make_async_copy(home_ref.at[others], home_ref.at[others], s_home).wait()
    pltpu.make_async_copy(back_ref.at[others], back_ref.at[others], s_back).wait()

    def widen(c, _):
        sums_ref[pl.ds(pl.multiple_of(c * ROWS, 8), ROWS), :] = home_ref[c].astype(F32)
        return 0

    lax.fori_loop(0, CHIPS, widen, 0, unroll=4)

    def finish(i, _):
        values = sums_ref[pl.ds(i, CHIPS, stride=ROWS), :]
        mean = jnp.mean(values, axis=0, keepdims=True)
        centred = values - mean
        spread = jnp.mean(centred * centred, axis=0, keepdims=True)
        normed = (centred * lax.rsqrt(spread + EPS) * gain_ref[...] + bias_ref[...]).astype(BF16)
        projected = dot(normed, w_out_ref[...], 0, 0)
        natural = jnp.concatenate([projected[0:24], projected[48:72], projected[24:48], projected[72:96]], axis=0)
        out_ref[i] = (gate_ref[i] * natural).astype(BF16)
        return 0

    lax.fori_loop(0, ROWS, finish, 0, unroll=4)


def shards(pair, tile_mask, chain_ids, in_gain, in_bias, w_ab, w_gate, out_gain, out_bias, w_out):
    args = (
        pair, tile_mask, chain_ids.reshape(6, 128), in_gain.reshape(1, C), in_bias.reshape(1, C), w_ab, w_gate,
        out_gain.reshape(1, C), out_bias.reshape(1, C), w_out,
    )
    return pl.pallas_call(
        kernel,
        out_shape=jax.ShapeDtypeStruct((ROWS, COLS, C), BF16),
        in_specs=[pl.BlockSpec(memory_space=pl.ANY)] * len(args),
        out_specs=pl.BlockSpec(memory_space=pltpu.VMEM),
        scratch_shapes=[pltpu.VMEM(arg.shape, arg.dtype) for arg in args]
        + [
            pltpu.VMEM((ROWS, COLS, C), BF16),
            pltpu.VMEM((TILES, 128, C), BF16),
            pltpu.VMEM((TILES, 128), F32),
            pltpu.VMEM((512, C), BF16),
            pltpu.VMEM((32 * MSG, 128), F32),
            pltpu.VMEM((CHIPS, MSG, 128), BF16),
            pltpu.VMEM((CHIPS, MSG, 128), BF16),
            pltpu.VMEM((ROWS, COLS, C), F32),
            pltpu.VMEM((4, 384, 256), BF16),
            pltpu.VMEM((4, 8, 128, 256), BF16),
            pltpu.VMEM((4, 384, 256), F32),
            pltpu.VMEM((CHIPS, ROWS, 128), BF16),
            pltpu.VMEM((CHIPS, ROWS, 128), BF16),
            pltpu.VMEM((CHIPS * ROWS, 128), F32),
            pltpu.VMEM((C, 128), F32),
            pltpu.VMEM((C, 128), F32),
            pltpu.SemaphoreType.DMA((len(args),)),
            pltpu.SemaphoreType.REGULAR,
            pltpu.SemaphoreType.REGULAR,
            pltpu.SemaphoreType.DMA(()),
            pltpu.SemaphoreType.DMA((4,)),
            pltpu.SemaphoreType.DMA((4,)),
            pltpu.SemaphoreType.DMA((4,)),
            pltpu.SemaphoreType.DMA(()),
            pltpu.SemaphoreType.DMA(()),
        ],
        compiler_params=pltpu.CompilerParams(collective_id=1, has_side_effects=True, vmem_limit_bytes=60 << 20),
    )(*args)


def solution(mesh):
    in_specs = (P("wide", "narrow", None), P(), P(), P(), P(), P(), P(), P(), P(), P())
    out_specs = P("wide", "narrow", None)
    return jax.shard_map(shards, mesh=mesh, in_specs=in_specs, out_specs=out_specs, check_vma=False)
```

time: 93.1 us -> 74.5 us (0.80)
  Pallas kernels: 87.1 us -> 72.4 us
  local copies, waits for them, and re-layouts: 5.61 us -> 1.92 us
    pallas_call x1, Pallas kernels: 87.1 us -> 72.4 us  [shards(): pl.pallas_call(kernel, out_shape=jax.ShapeDtypeStruct((ROWS, COLS, C), BF...]
    unnamed x17 -> x1, local copies, waits for them, and re-layouts: 4.1 us -> 1.92 us
    broadcast_in_dim x2 -> x0, local copies, waits for them, and re-layouts: 1.51 us -> none  [the longest x1 0.76 us: shards(): jnp.broadcast_to(out_gain[:, None], (C, 128))]
where the time goes in v2:
time: 74.5 us; the launch traced here: 74.3 us
  Pallas kernels  72.4 us (97%)
  local copies, waits for them, and re-layouts  1.92 us (3%)
    pallas_call x1, Pallas kernels, shards(): pl.pallas_call(kernel, out_shape=jax.ShapeDtypeStruct((ROWS, COLS, C), BF...  72.4 us
    unnamed x1, local copies, waits for them, and re-layouts  1.92 us

profile of v2, /device:TPU:1, one launch (start us, length us, event | category | flops | bytes accessed | tf_op | source)
XLA Modules:
  0.0 74.3 jit_solution(2478678089293719510)
XLA Ops:
  0.0 72.4 %shard_map.100 = bf16[24,96,128]{2,1,0:T(8,128)(2,1)} custom-call(bf16[24,96,128]{2,1,0:T(8,128)(2,1)} %pair_hbm.1, s32[6,6]{1,0:T(8,128)} %tile_hbm.1, s32[6,128]{1,0:T(8,128)} %bitcast.5, f32[1,128]{1,0:T(1,128)} %bitcast.6, f32[1,128]{1,0:T(1,128)} %bitcast.7, bf16[128,512]{1,0:T(8,128)(2,1)} %w_ab_hbm.1, bf16[128,128]{1,0:T(8,128)(2,1)} %w_gate_hbm.1, ...), custom_call_target="tpu_custom_call" | custom-call | tf_op jit(solution)/shard_map/pallas_call | solution.py:318
  72.4 1.9 %copy.12 = bf16[24,96,128]{2,1,0:T(8,128)(2,1)} copy(bf16[24,96,128]{2,1,0:T(8,128)(2,1)} %shard_map.100) | data formatting | bytes 1179648

commit v3 on v2

--- a/solution.py
+++ b/solution.py
@@ -11,8 +11,9 @@
 F32, BF16 = jnp.float32, jnp.bfloat16
 CHIPS = 128
 ROWS, COLS, C = 24, 96, 128
-MSG = 40
-TILES = 24
+MSG, SLOT = 36, 48
+BACK, HOME = 18, 32
+TILES = 18
 EPS = 1e-05
 
 
@@ -28,7 +29,7 @@
     tile = lax.broadcasted_iota(jnp.int32, (TILES, 128), 0)
     lane = lax.broadcasted_iota(jnp.int32, (TILES, 128), 1)
     body, main = tile < 16, lane < 96
-    i = jnp.where(body & jnp.logical_not(main), 16 + tile % 8, tile)
+    i = jnp.where(body, jnp.where(main, tile, 16 + tile % 8), 16 + 4 * (tile - 16) + lane // 32)
     k = jnp.where(body, jnp.where(main, lane, lane - 96 + 32 * (tile // 8)), 64 + lane % 32)
     i = i + wide * ROWS
     k = k + narrow * COLS
@@ -118,9 +119,7 @@
         normed = norm_row(16 + r)
         packed_ref[r, 96:128] = normed[0:32]
         packed_ref[8 + r, 96:128] = normed[32:64]
-        last = normed[64:96]
-        for q in range(4):
-            packed_ref[16 + r, 32 * q : 32 * q + 32] = last
+        packed_ref[16 + r // 4, pl.ds(pl.multiple_of(32 * (r % 4), 32), 32)] = normed[64:96]
         return 0
 
     lax.fori_loop(0, 16, norm_body, 0, unroll=2)
@@ -130,7 +129,7 @@
     for device in line_x:
         pl.semaphore_signal(s_plane, inc=1, device_id=device, device_id_type=MESH)
 
-    lane32 = lax.broadcasted_iota(jnp.int32, (32, 128), 1)
+    used = pl.ds(0, MSG)
 
     def send_chunk(dx):
         px = (x + dx) % 4
@@ -151,28 +150,24 @@
         def project(h, _):
             t = 2 * h
             for q, (left, right) in enumerate(sides(t)):
-                stage_ref[pl.ds(t + q, 32, stride=MSG), :] = left
-                stage_ref[pl.ds(16 + t + q, 32, stride=MSG), :] = right
-            return 0
-
-        def project_tail(h, _):
-            t = 2 * h
-            for q, (left, right) in enumerate(sides(t)):
-                stage_ref[pl.ds(16 + t + q, 32, stride=MSG), :] = jnp.where(lane32 < 32, left, right)
+                stage_ref[pl.ds(t + q, 32, stride=SLOT), :] = left
+                stage_ref[pl.ds(16 + t + q, 32, stride=SLOT), :] = right
             return 0
 
         lax.fori_loop(0, 8, project, 0, unroll=2)
-        lax.fori_loop(8, 12, project_tail, 0, unroll=2)
+        for q, (left, right) in enumerate(sides(16)):
+            stage_ref[pl.ds(32 + q, 32, stride=SLOT), :] = left
+            stage_ref[pl.ds(34 + q, 32, stride=SLOT), :] = right
 
         def cast(c):
-            start = pl.multiple_of(c * MSG, 8)
-            send_ref[px * 32 + c] = stage_ref[pl.ds(start, MSG), :].astype(BF16)
+            start = pl.multiple_of(c * SLOT, 16)
+            send_ref[px * 32 + c] = stage_ref[pl.ds(start, SLOT), :].astype(BF16)
 
         def send(d, _):
             py, pz = (y + d // 8) % 4, (z + d % 8) % 8
             slot = px * 32 + py * 8 + pz
             pltpu.make_async_remote_copy(
-                src_ref=send_ref.at[slot], dst_ref=recv_ref.at[me], send_sem=s_send, recv_sem=s_recv.at[dx],
+                src_ref=send_ref.at[slot, used], dst_ref=recv_ref.at[me, used], send_sem=s_send, recv_sem=s_recv.at[dx],
                 device_id=device_at(px, py, pz), device_id_type=MESH,
             ).start()
             return 0
@@ -183,10 +178,13 @@
 
         lax.fori_loop(0, 32, cast_body, 0, unroll=4)
         if dx == 0:
-            pl.semaphore_wait(s_plane, len(line_x))
-        lax.fori_loop(1 if dx == 0 else 0, 32, send, 0)
-        if dx == 0:
+            lax.fori_loop(1, 8, send, 0)
+            lax.fori_loop(8, 32, send, 0)
             recv_ref[me] = send_ref[me]
+        else:
+            if dx == 1:
+                pl.semaphore_wait(s_plane, len(line_x))
+            lax.fori_loop(0, 32, send, 0)
 
     for dx in range(4):
         send_chunk(dx)
@@ -201,20 +199,25 @@
             b_ref[dx, p, 96:128] = jnp.zeros((32, 256), BF16)
 
     lane = lax.broadcasted_iota(jnp.int32, (8, 128), 1)
+    row = lax.broadcasted_iota(jnp.int32, (8, 128), 0)
 
     def unpack(slot):
         f = recv_ref[slot].astype(F32)
-        low = f[32:40]
         zero = jnp.zeros((8, 128), F32)
 
-        def rest(top, middle, shift):
+        def rest(top, middle, at):
+            low = jnp.where(row < 4, f[at : at + 1], f[at + 1 : at + 2])
+            turned = [pltpu.roll(low, 64, 1), pltpu.roll(low, 32, 1), low, pltpu.roll(low, 96, 1)]
+            low = turned[3]
+            for q in range(3):
+                low = jnp.where(row % 4 == q, turned[q], low)
             return jnp.where(
                 lane < 32, pltpu.roll(top, 32, 1),
-                jnp.where(lane < 64, pltpu.roll(middle, 64, 1), jnp.where(lane < 96, pltpu.roll(low, shift, 1), zero)),
+                jnp.where(lane < 64, pltpu.roll(middle, 64, 1), jnp.where(lane < 96, low, zero)),
             )
 
-        left = [jnp.where(lane < 96, f[0:8], zero), jnp.where(lane < 96, f[8:16], zero), rest(f[0:8], f[8:16], 64)]
-        right = [f[16:24], f[24:32], rest(f[16:24], f[24:32], 32)]
+        left = [jnp.where(lane < 96, f[0:8], zero), jnp.where(lane < 96, f[8:16], zero), rest(f[0:8], f[8:16], 32)]
+        right = [f[16:24], f[24:32], rest(f[16:24], f[24:32], 34)]
         return left, right
 
     mine = pl.ds(pl.multiple_of(core * 48, 16), 48)
@@ -227,7 +230,7 @@
         )
 
     def receive(dx):
-        arrived = recv_ref.at[pl.ds(0, 31 if dx == 0 else 32)]
+        arrived = recv_ref.at[pl.ds(0, 31 if dx == 0 else 32), used]
         pltpu.make_async_copy(arrived, arrived, s_recv.at[dx]).wait()
         first = ((x + 4 - dx) % 4) * 32
 
@@ -265,17 +268,32 @@
             multiply(dx - 1)
     swap(3).wait()
 
+    def pack(block):
+        extra = block[16:24]
+        top = jnp.where(lane < 96, block[0:8], pltpu.roll(extra, 96, 1))
+        middle = jnp.where(lane < 96, block[8:16], pltpu.roll(extra, 64, 1))
+        turned = [pltpu.roll(extra, 64, 1), pltpu.roll(extra, 96, 1), extra, pltpu.roll(extra, 32, 1)]
+        spread = jnp.zeros((8, 128), F32)
+        for q in range(4):
+            spread = jnp.where((row % 4 == q) & (lane // 32 == q), turned[q], spread)
+        first = jnp.sum(spread[0:4], axis=0, keepdims=True)
+        second = jnp.sum(spread[4:8], axis=0, keepdims=True)
+        low = jnp.where(row == 0, first, second)
+        return jnp.concatenate([top, middle, low, low], axis=0).astype(BF16)
+
+    sent = pl.ds(0, BACK)
+
     def back(q, _):
         px = (x + q) % 4
-        product = (total_ref[px] + partial(3, px)).astype(BF16)
+        product = total_ref[px] + partial(3, px)
         for h in range(2):
             for w in range(16):
-                back_ref[px * 32 + h * 16 + w] = product[24 * w : 24 * w + 24, 128 * h : 128 * h + 128]
+                back_ref[px * 32 + h * 16 + w] = pack(product[24 * w : 24 * w + 24, 128 * h : 128 * h + 128])
 
         def send(d, _):
             py, pz = (y + d // 8) % 4, (z + d % 8) % 8
             pltpu.make_async_remote_copy(
-                src_ref=back_ref.at[px * 32 + py * 8 + pz], dst_ref=home_ref.at[me], send_sem=s_back, recv_sem=s_home,
+                src_ref=back_ref.at[px * 32 + py * 8 + pz, sent], dst_ref=home_ref.at[me, sent], send_sem=s_back, recv_sem=s_home,
                 device_id=device_at(px, py, pz), device_id_type=MESH,
             ).start()
             return 0
@@ -286,18 +304,33 @@
     lax.fori_loop(0, 4, back, 0)
     home_ref[me] = back_ref[me]
     others = pl.ds(0, CHIPS - 1)
-    pltpu.make_async_copy(send_ref.at[others], send_ref.at[others], s_send).wait()
-    pltpu.make_async_copy(home_ref.at[others], home_ref.at[others], s_home).wait()
-    pltpu.make_async_copy(back_ref.at[others], back_ref.at[others], s_back).wait()
+    pltpu.make_async_copy(send_ref.at[others, used], send_ref.at[others, used], s_send).wait()
+    pltpu.make_async_copy(home_ref.at[others, sent], home_ref.at[others, sent], s_home).wait()
+    pltpu.make_async_copy(back_ref.at[others, sent], back_ref.at[others, sent], s_back).wait()
 
     def widen(c, _):
-        sums_ref[pl.ds(pl.multiple_of(c * ROWS, 8), ROWS), :] = home_ref[c].astype(F32)
+        sums_ref[pl.ds(pl.multiple_of(c * ROWS, 8), ROWS), :] = home_ref[c].astype(F32)[0:ROWS]
         return 0
 
     lax.fori_loop(0, CHIPS, widen, 0, unroll=4)
 
-    def finish(i, _):
-        values = sums_ref[pl.ds(i, CHIPS, stride=ROWS), :]
+    lanes = lax.broadcasted_iota(jnp.int32, (CHIPS, 128), 1)
+
+    def rows_at(at):
+        return sums_ref[pl.ds(at, CHIPS, stride=ROWS), :]
+
+    def finish_main(i, _):
+        finish(i, rows_at(i))
+        return 0
+
+    def finish_rest(r, q):
+        low = rows_at(16 + r // 4)
+        shift = (64 - 32 * q) % 128
+        low = pltpu.roll(low, shift, 1) if shift else low
+        high = jnp.where(lanes < 32, pltpu.roll(rows_at(r), 32, 1), pltpu.roll(rows_at(8 + r), 64, 1))
+        finish(16 + r, jnp.where(lanes < 64, high, low))
+
+    def finish(i, values):
         mean = jnp.mean(values, axis=0, keepdims=True)
         centred = values - mean
         spread = jnp.mean(centred * centred, axis=0, keepdims=True)
@@ -305,9 +338,15 @@
         projected = dot(normed, w_out_ref[...], 0, 0)
         natural = jnp.concatenate([projected[0:24], projected[48:72], projected[24:48], projected[72:96]], axis=0)
         out_ref[i] = (gate_ref[i] * natural).astype(BF16)
-        return 0
-
-    lax.fori_loop(0, ROWS, finish, 0, unroll=4)
+
+    lax.fori_loop(0, 16, finish_main, 0, unroll=4)
+
+    def finish_four(h, _):
+        for q in range(4):
+            finish_rest(4 * h + q, q)
+        return 0
+
+    lax.fori_loop(0, 2, finish_four, 0)
 
 
 def shards(pair, tile_mask, chain_ids, in_gain, in_bias, w_ab, w_gate, out_gain, out_bias, w_out):
@@ -318,7 +357,7 @@
     return pl.pallas_call(
         kernel,
         out_shape=jax.ShapeDtypeStruct((ROWS, COLS, C), BF16),
-        in_specs=[pl.BlockSpec(memory_space=pl.ANY)] * len(args),
+        in_specs=[pl.BlockSpec(memory_space=pltpu.HBM)] * len(args),
         out_specs=pl.BlockSpec(memory_space=pltpu.VMEM),
         scratch_shapes=[pltpu.VMEM(arg.shape, arg.dtype) for arg in args]
         + [
@@ -326,15 +365,15 @@
             pltpu.VMEM((TILES, 128, C), BF16),
             pltpu.VMEM((TILES, 128), F32),
             pltpu.VMEM((512, C), BF16),
-            pltpu.VMEM((32 * MSG, 128), F32),
-            pltpu.VMEM((CHIPS, MSG, 128), BF16),
-            pltpu.VMEM((CHIPS, MSG, 128), BF16),
+            pltpu.VMEM((32 * SLOT, 128), F32),
+            pltpu.VMEM((CHIPS, SLOT, 128), BF16),
+            pltpu.VMEM((CHIPS, SLOT, 128), BF16),
             pltpu.VMEM((ROWS, COLS, C), F32),
             pltpu.VMEM((4, 384, 256), BF16),
             pltpu.VMEM((4, 8, 128, 256), BF16),
             pltpu.VMEM((4, 384, 256), F32),
-            pltpu.VMEM((CHIPS, ROWS, 128), BF16),
-            pltpu.VMEM((CHIPS, ROWS, 128), BF16),
+            pltpu.VMEM((CHIPS, HOME, 128), BF16),
+            pltpu.VMEM((CHIPS, HOME, 128), BF16),
             pltpu.VMEM((CHIPS * ROWS, 128), F32),
             pltpu.VMEM((C, 128), F32),
             pltpu.VMEM((C, 128), F32),

time: 74.5 us -> 68.6 us (0.921)
  Pallas kernels: 72.4 us -> 66.6 us
    pallas_call x1, Pallas kernels: 72.4 us -> 66.6 us  [shards(): pl.pallas_call(kernel, out_shape=jax.ShapeDtypeStruct((ROWS, COLS, C), BF...]
where the time goes in v3:
time: 68.6 us; the launch traced here: 68.5 us
  Pallas kernels  66.6 us (97%)
  local copies, waits for them, and re-layouts  1.92 us (3%)
    pallas_call x1, Pallas kernels, shards(): pl.pallas_call(kernel, out_shape=jax.ShapeDtypeStruct((ROWS, COLS, C), BF...  66.6 us
    unnamed x1, local copies, waits for them, and re-layouts  1.92 us

profile of v3, /device:TPU:1, one launch (start us, length us, event | category | flops | bytes accessed | tf_op | source)
XLA Modules:
  0.0 68.5 jit_solution(771742063035406596)
XLA Ops:
  0.0 66.6 %shard_map.100 = bf16[24,96,128]{2,1,0:T(8,128)(2,1)} custom-call(bf16[24,96,128]{2,1,0:T(8,128)(2,1)} %pair_hbm.1, s32[6,6]{1,0:T(8,128)} %tile_hbm.1, s32[6,128]{1,0:T(8,128)} %bitcast.5, f32[1,128]{1,0:T(1,128)} %bitcast.6, f32[1,128]{1,0:T(1,128)} %bitcast.7, bf16[128,512]{1,0:T(8,128)(2,1)} %w_ab_hbm.1, bf16[128,128]{1,0:T(8,128)(2,1)} %w_gate_hbm.1, ...), custom_call_target="tpu_custom_call" | custom-call | tf_op jit(solution)/shard_map/pallas_call | solution.py:357
  66.6 1.9 %copy.12 = bf16[24,96,128]{2,1,0:T(8,128)(2,1)} copy(bf16[24,96,128]{2,1,0:T(8,128)(2,1)} %shard_map.100) | data formatting | bytes 1179648

commit v4 on v3

--- a/solution.py
+++ b/solution.py
@@ -95,16 +95,11 @@
 
     w_t_ref[...] = w_ab_ref[...].T
     mask_ref[...] = keep_mask(wide, narrow, tile_ref, chain_ref)
-    gain_ref[...] = jnp.broadcast_to(out_gain_ref[...], (C, 128)).T
-    bias_ref[...] = jnp.broadcast_to(out_bias_ref[...], (C, 128)).T
-
-    pl.semaphore_wait(barrier, len(greeted))
-    for device in line_y:
-        pl.semaphore_signal(s_line, inc=1, device_id=device, device_id_type=MESH)
+    ones = jnp.ones((C, 128), BF16)
 
     def norm_row(i):
         values = pair_ref[i].astype(F32)
-        mean = jnp.mean(values, axis=1, keepdims=True)
+        mean = dot(pair_ref[i], ones, 1, 0) * (1.0 / C)
         centred = values - mean
         spread = jnp.mean(centred * centred, axis=1, keepdims=True)
         normed = (centred * lax.rsqrt(spread + EPS) * in_gain_ref[...] + in_bias_ref[...]).astype(BF16)
@@ -122,12 +117,12 @@
         packed_ref[16 + r // 4, pl.ds(pl.multiple_of(32 * (r % 4), 32), 32)] = normed[64:96]
         return 0
 
-    lax.fori_loop(0, 16, norm_body, 0, unroll=2)
-    lax.fori_loop(0, 8, norm_tail, 0, unroll=2)
-
-    pl.semaphore_wait(s_line, len(line_y))
-    for device in line_x:
-        pl.semaphore_signal(s_plane, inc=1, device_id=device, device_id_type=MESH)
+    lax.fori_loop(0, 16, norm_body, 0, unroll=4)
+    lax.fori_loop(0, 8, norm_tail, 0, unroll=4)
+
+    pl.semaphore_wait(barrier, len(greeted))
+    for device in line_y:
+        pl.semaphore_signal(s_line, inc=1, device_id=device, device_id_type=MESH)
 
     used = pl.ds(0, MSG)
 
@@ -179,6 +174,9 @@
         lax.fori_loop(0, 32, cast_body, 0, unroll=4)
         if dx == 0:
             lax.fori_loop(1, 8, send, 0)
+            pl.semaphore_wait(s_line, len(line_y))
+            for device in line_x:
+                pl.semaphore_signal(s_plane, inc=1, device_id=device, device_id_type=MESH)
             lax.fori_loop(8, 32, send, 0)
             recv_ref[me] = send_ref[me]
         else:
@@ -193,7 +191,9 @@
         gate_ref[i] = sigmoid(dot(normed_ref[i], w_gate_ref[...], 1, 0))
         return 0
 
-    lax.fori_loop(0, ROWS, gates, 0)
+    lax.fori_loop(0, ROWS, gates, 0, unroll=2)
+    gain_ref[...] = jnp.broadcast_to(out_gain_ref[...], (C, 128)).T
+    bias_ref[...] = jnp.broadcast_to(out_bias_ref[...], (C, 128)).T
     for dx in range(4):
         for p in range(8):
             b_ref[dx, p, 96:128] = jnp.zeros((32, 256), BF16)
@@ -293,7 +293,7 @@
         def send(d, _):
             py, pz = (y + d // 8) % 4, (z + d % 8) % 8
             pltpu.make_async_remote_copy(
-                src_ref=back_ref.at[px * 32 + py * 8 + pz, sent], dst_ref=home_ref.at[me, sent], send_sem=s_back, recv_sem=s_home,
+                src_ref=back_ref.at[px * 32 + py * 8 + pz, sent], dst_ref=home_ref.at[me, sent], send_sem=s_back, recv_sem=s_home.at[q],
                 device_id=device_at(px, py, pz), device_id_type=MESH,
             ).start()
             return 0
@@ -305,14 +305,16 @@
     home_ref[me] = back_ref[me]
     others = pl.ds(0, CHIPS - 1)
     pltpu.make_async_copy(send_ref.at[others, used], send_ref.at[others, used], s_send).wait()
-    pltpu.make_async_copy(home_ref.at[others, sent], home_ref.at[others, sent], s_home).wait()
-    pltpu.make_async_copy(back_ref.at[others, sent], back_ref.at[others, sent], s_back).wait()
 
     def widen(c, _):
         sums_ref[pl.ds(pl.multiple_of(c * ROWS, 8), ROWS), :] = home_ref[c].astype(F32)[0:ROWS]
         return 0
 
-    lax.fori_loop(0, CHIPS, widen, 0, unroll=4)
+    for q in range(4):
+        arrived = home_ref.at[pl.ds(0, 31 if q == 0 else 32), sent]
+        pltpu.make_async_copy(arrived, arrived, s_home.at[q]).wait()
+        first = ((x + 4 - q) % 4) * 32
+        lax.fori_loop(0, 32, lambda c, _, first=first: widen(first + c, _), 0, unroll=4)
 
     lanes = lax.broadcasted_iota(jnp.int32, (CHIPS, 128), 1)
 
@@ -347,6 +349,7 @@
         return 0
 
     lax.fori_loop(0, 2, finish_four, 0)
+    pltpu.make_async_copy(back_ref.at[others, sent], back_ref.at[others, sent], s_back).wait()
 
 
 def shards(pair, tile_mask, chain_ids, in_gain, in_bias, w_ab, w_gate, out_gain, out_bias, w_out):
@@ -354,9 +357,10 @@
         pair, tile_mask, chain_ids.reshape(6, 128), in_gain.reshape(1, C), in_bias.reshape(1, C), w_ab, w_gate,
         out_gain.reshape(1, C), out_bias.reshape(1, C), w_out,
     )
+    args = tuple(pltpu.with_memory_space_constraint(arg, pltpu.HBM) for arg in args)
     return pl.pallas_call(
         kernel,
-        out_shape=jax.ShapeDtypeStruct((ROWS, COLS, C), BF16),
+        out_shape=pltpu.VMEM((ROWS, COLS, C), BF16),
         in_specs=[pl.BlockSpec(memory_space=pltpu.HBM)] * len(args),
         out_specs=pl.BlockSpec(memory_space=pltpu.VMEM),
         scratch_shapes=[pltpu.VMEM(arg.shape, arg.dtype) for arg in args]
@@ -385,9 +389,9 @@
             pltpu.SemaphoreType.DMA((4,)),
             pltpu.SemaphoreType.DMA((4,)),
             pltpu.SemaphoreType.DMA(()),
-            pltpu.SemaphoreType.DMA(()),
+            pltpu.SemaphoreType.DMA((4,)),
         ],
-        compiler_params=pltpu.CompilerParams(collective_id=1, has_side_effects=True, vmem_limit_bytes=60 << 20),
+        compiler_params=pltpu.CompilerParams(collective_id=1, has_side_effects=True, vmem_limit_bytes=40 << 20),
     )(*args)
 
 

time: 68.6 us -> 63.9 us (0.931)
  Pallas kernels: 66.6 us -> 63 us
  local copies, waits for them, and re-layouts: 1.92 us -> 0.82 us
    pallas_call x1, Pallas kernels: 66.6 us -> 63 us  [shards(): pl.pallas_call(kernel, out_shape=pltpu.VMEM((ROWS, COLS, C), BF16), in_sp...]
    unnamed x1, local copies, waits for them, and re-layouts: 1.92 us -> 0.82 us
where the time goes in v4:
time: 63.9 us
  Pallas kernels  63 us (99%)
  local copies, waits for them, and re-layouts  0.82 us (1%)
    pallas_call x1, Pallas kernels, shards(): pl.pallas_call(kernel, out_shape=pltpu.VMEM((ROWS, COLS, C), BF16), in_sp...  63 us

profile of v4, /device:TPU:1, one launch (start us, length us, event | category | flops | bytes accessed | tf_op | source)
XLA Modules:
  0.0 63.9 jit_solution(13779599253611354257)
XLA Ops:
  0.0 63.0 %shard_map.100 = bf16[24,96,128]{2,1,0:T(8,128)(2,1)S(1)} custom-call(bf16[24,96,128]{2,1,0:T(8,128)(2,1)} %pair_hbm.1, s32[6,6]{1,0:T(8,128)} %tile_hbm.1, s32[6,128]{1,0:T(8,128)} %bitcast.5, f32[1,128]{1,0:T(1,128)} %bitcast.6, f32[1,128]{1,0:T(1,128)} %bitcast.7, bf16[128,512]{1,0:T(8,128)(2,1)} %w_ab_hbm.1, bf16[128,128]{1,0:T(8,128)(2,1)} %w_gate_hbm.1, ...), custom_call_target="tpu_custom_call" | custom-call | tf_op jit(solution)/shard_map/pallas_call | solution.py:361
  63.0 0.8 %copy.12 = bf16[24,96,128]{2,1,0:T(8,128)(2,1)} copy(bf16[24,96,128]{2,1,0:T(8,128)(2,1)S(1)} %shard_map.100) | data formatting | bytes 1179648

commit v5 on v4

--- a/solution.py
+++ b/solution.py
@@ -11,9 +11,9 @@
 F32, BF16 = jnp.float32, jnp.bfloat16
 CHIPS = 128
 ROWS, COLS, C = 24, 96, 128
-MSG, SLOT = 36, 48
-BACK, HOME = 18, 32
+MSG, SLOT, STAGE = 18, 32, 48
 TILES = 18
+PAIRS = ((3, 5), (0, 4), (2, 6), (1, 7))
 EPS = 1e-05
 
 
@@ -56,9 +56,9 @@
     pair_hbm, tile_hbm, chain_hbm, in_gain_hbm, in_bias_hbm, w_ab_hbm, w_gate_hbm, out_gain_hbm, out_bias_hbm, w_out_hbm,
     out_ref,
     pair_ref, tile_ref, chain_ref, in_gain_ref, in_bias_ref, w_ab_ref, w_gate_ref, out_gain_ref, out_bias_ref, w_out_ref,
-    normed_ref, packed_ref, mask_ref, w_t_ref, stage_ref, send_ref, recv_ref, gate_ref, a_ref, b_ref, total_ref, back_ref,
-    home_ref, sums_ref, gain_ref, bias_ref,
-    s_in, s_line, s_plane, s_send, s_recv, s_swap_send, s_swap_recv, s_back, s_home,
+    normed_ref, packed_ref, mask_ref, w_t_ref, stage_ref, left_out, right_out, left_in, right_in, gate_ref, a_ref, b_ref,
+    back_ref, home_ref, sums_ref, gain_ref, bias_ref,
+    s_in, s_line, s_plane, s_left_out, s_right_out, s_left_in, s_right_in, s_swap_send, s_swap_recv, s_back, s_home,
 ):
     wide, narrow = lax.axis_index("wide"), lax.axis_index("narrow")
     w16, core = wide // 2, wide % 2
@@ -145,25 +145,23 @@
         def project(h, _):
             t = 2 * h
             for q, (left, right) in enumerate(sides(t)):
-                stage_ref[pl.ds(t + q, 32, stride=SLOT), :] = left
-                stage_ref[pl.ds(16 + t + q, 32, stride=SLOT), :] = right
-            return 0
-
-        lax.fori_loop(0, 8, project, 0, unroll=2)
-        for q, (left, right) in enumerate(sides(16)):
-            stage_ref[pl.ds(32 + q, 32, stride=SLOT), :] = left
-            stage_ref[pl.ds(34 + q, 32, stride=SLOT), :] = right
+                stage_ref[pl.ds(t + q, 32, stride=STAGE), :] = left
+                stage_ref[pl.ds(24 + t + q, 32, stride=STAGE), :] = right
+            return 0
+
+        lax.fori_loop(0, TILES // 2, project, 0, unroll=3)
 
         def cast(c):
-            start = pl.multiple_of(c * SLOT, 16)
-            send_ref[px * 32 + c] = stage_ref[pl.ds(start, SLOT), :].astype(BF16)
+            start = pl.multiple_of(c * STAGE, 16)
+            both = stage_ref[pl.ds(start, STAGE), :]
+            left_out[px * 32 + c] = both[0:32].astype(BF16)
+            right_out[px * 32 + c] = jnp.concatenate([both[24:48], both[40:48]], axis=0).astype(BF16)
 
         def send(d, _):
             py, pz = (y + d // 8) % 4, (z + d % 8) % 8
-            slot = px * 32 + py * 8 + pz
             pltpu.make_async_remote_copy(
-                src_ref=send_ref.at[slot, used], dst_ref=recv_ref.at[me, used], send_sem=s_send, recv_sem=s_recv.at[dx],
-                device_id=device_at(px, py, pz), device_id_type=MESH,
+                src_ref=right_out.at[px * 32 + py * 8 + pz, used], dst_ref=right_in.at[me, used], send_sem=s_right_out,
+                recv_sem=s_right_in.at[dx], device_id=device_at(px, py, pz), device_id_type=MESH,
             ).start()
             return 0
 
@@ -178,7 +176,6 @@
             for device in line_x:
                 pl.semaphore_signal(s_plane, inc=1, device_id=device, device_id_type=MESH)
             lax.fori_loop(8, 32, send, 0)
-            recv_ref[me] = send_ref[me]
         else:
             if dx == 1:
                 pl.semaphore_wait(s_plane, len(line_x))
@@ -187,6 +184,25 @@
     for dx in range(4):
         send_chunk(dx)
 
+    def send_pair(source, target, s_out, s_in_pair, pair, sign):
+        for dz in pair:
+            pz = (z + sign * dz + 8) % 8
+
+            def send(r, _, pz=pz):
+                px, py = (x + r // 4) % 4, (y + r % 4) % 4
+                pltpu.make_async_remote_copy(
+                    src_ref=source.at[px * 32 + py * 8 + pz, used], dst_ref=target.at[me, used], send_sem=s_out,
+                    recv_sem=s_in_pair, device_id=device_at(px, py, pz), device_id_type=MESH,
+                ).start()
+                return 0
+
+            lax.fori_loop(1 if dz == 0 else 0, 16, send, 0)
+
+    for at, pair in enumerate(PAIRS):
+        send_pair(left_out, left_in, s_left_out, s_left_in.at[at], pair, 1)
+    left_in[me] = left_out[me]
+    right_in[me] = right_out[me]
+
     def gates(i, _):
         gate_ref[i] = sigmoid(dot(normed_ref[i], w_gate_ref[...], 1, 0))
         return 0
@@ -194,79 +210,54 @@
     lax.fori_loop(0, ROWS, gates, 0, unroll=2)
     gain_ref[...] = jnp.broadcast_to(out_gain_ref[...], (C, 128)).T
     bias_ref[...] = jnp.broadcast_to(out_bias_ref[...], (C, 128)).T
-    for dx in range(4):
-        for p in range(8):
-            b_ref[dx, p, 96:128] = jnp.zeros((32, 256), BF16)
+    for p in range(8):
+        b_ref[p, 96:128] = jnp.zeros((32, 1024), BF16)
 
     lane = lax.broadcasted_iota(jnp.int32, (8, 128), 1)
     row = lax.broadcasted_iota(jnp.int32, (8, 128), 0)
 
-    def unpack(slot):
-        f = recv_ref[slot].astype(F32)
+    def unpack(ref, slot, last):
+        f = ref[slot].astype(F32)
+        low = jnp.where(row < 4, f[16:17], f[17:18])
+        turned = [pltpu.roll(low, 64, 1), pltpu.roll(low, 32, 1), low, pltpu.roll(low, 96, 1)]
+        low = turned[3]
+        for q in range(3):
+            low = jnp.where(row % 4 == q, turned[q], low)
+        rest = jnp.where(lane < 32, pltpu.roll(f[0:8], 32, 1), jnp.where(lane < 64, pltpu.roll(f[8:16], 64, 1), low))
+        if last:
+            return [f[0:8], f[8:16], rest]
         zero = jnp.zeros((8, 128), F32)
-
-        def rest(top, middle, at):
-            low = jnp.where(row < 4, f[at : at + 1], f[at + 1 : at + 2])
-            turned = [pltpu.roll(low, 64, 1), pltpu.roll(low, 32, 1), low, pltpu.roll(low, 96, 1)]
-            low = turned[3]
-            for q in range(3):
-                low = jnp.where(row % 4 == q, turned[q], low)
-            return jnp.where(
-                lane < 32, pltpu.roll(top, 32, 1),
-                jnp.where(lane < 64, pltpu.roll(middle, 64, 1), jnp.where(lane < 96, low, zero)),
-            )
-
-        left = [jnp.where(lane < 96, f[0:8], zero), jnp.where(lane < 96, f[8:16], zero), rest(f[0:8], f[8:16], 32)]
-        right = [f[16:24], f[24:32], rest(f[16:24], f[24:32], 34)]
-        return left, right
+        return [jnp.where(lane < 96, part, zero) for part in (f[0:8], f[8:16], rest)]
 
     mine = pl.ds(pl.multiple_of(core * 48, 16), 48)
 
     def swap(dx):
-        half = b_ref.at[dx, :, mine, :]
+        half = b_ref.at[:, mine, 256 * dx : 256 * dx + 256]
         return pltpu.make_async_remote_copy(
             src_ref=half, dst_ref=half, send_sem=s_swap_send.at[dx], recv_sem=s_swap_recv.at[dx], device_id=sibling,
             device_id_type=MESH,
         )
 
-    def receive(dx):
-        arrived = recv_ref.at[pl.ds(0, 31 if dx == 0 else 32), used]
-        pltpu.make_async_copy(arrived, arrived, s_recv.at[dx]).wait()
+    def receive_right(dx):
+        arrived = right_in.at[pl.ds(0, 31 if dx == 0 else 32), used]
+        pltpu.make_async_copy(arrived, arrived, s_right_in.at[dx]).wait()
         first = ((x + 4 - dx) % 4) * 32
 
         def assemble(p, _):
             for q in range(2):
-                left0, right0 = unpack(first + 16 * q + 2 * p)
-                left1, right1 = unpack(first + 16 * q + 2 * p + 1)
-                columns = slice(128 * q, 128 * q + 128)
-                rows = pl.ds(pl.multiple_of(p * 48, 16), 48)
-                a_ref[dx, rows, columns] = jnp.concatenate(left0 + left1, axis=0).astype(BF16)
-                b_ref[dx, p, mine, columns] = jnp.concatenate(right0 + right1, axis=0).astype(BF16)
+                right0 = unpack(right_in, first + 16 * q + 2 * p, True)
+                right1 = unpack(right_in, first + 16 * q + 2 * p + 1, True)
+                columns = slice(256 * dx + 128 * q, 256 * dx + 128 * q + 128)
+                b_ref[p, mine, columns] = jnp.concatenate(right0 + right1, axis=0).astype(BF16)
             return 0
 
         lax.fori_loop(0, 8, assemble, 0)
         swap(dx).start()
 
-    def partial(dx, px):
-        return dot(a_ref[dx], b_ref[dx, pl.ds(2 * px, 2)].reshape(256, 256), 1, 1)
-
-    def multiply(dx):
+    for dx in range(4):
+        receive_right(dx)
+    for dx in range(4):
         swap(dx).wait()
-
-        def step(px, _):
-            if dx == 0:
-                total_ref[px] = partial(dx, px)
-            else:
-                total_ref[px] += partial(dx, px)
-            return 0
-
-        lax.fori_loop(0, 4, step, 0)
-
-    for dx in range(4):
-        receive(dx)
-        if dx > 0:
-            multiply(dx - 1)
-    swap(3).wait()
 
     def pack(block):
         extra = block[16:24]
@@ -281,40 +272,52 @@
         low = jnp.where(row == 0, first, second)
         return jnp.concatenate([top, middle, low, low], axis=0).astype(BF16)
 
-    sent = pl.ds(0, BACK)
-
-    def back(q, _):
-        px = (x + q) % 4
-        product = total_ref[px] + partial(3, px)
-        for h in range(2):
-            for w in range(16):
-                back_ref[px * 32 + h * 16 + w] = pack(product[24 * w : 24 * w + 24, 128 * h : 128 * h + 128])
-
-        def send(d, _):
-            py, pz = (y + d // 8) % 4, (z + d % 8) % 8
-            pltpu.make_async_remote_copy(
-                src_ref=back_ref.at[px * 32 + py * 8 + pz, sent], dst_ref=home_ref.at[me, sent], send_sem=s_back, recv_sem=s_home.at[q],
-                device_id=device_at(px, py, pz), device_id_type=MESH,
-            ).start()
-            return 0
-
-        lax.fori_loop(jnp.where(q == 0, 1, 0), 32, send, 0)
-        return 0
-
-    lax.fori_loop(0, 4, back, 0)
+    def multiply(at, pair):
+        arrived = left_in.at[pl.ds(0, 31 if pair[0] == 0 else 32), used]
+        pltpu.make_async_copy(arrived, arrived, s_left_in.at[at]).wait()
+        places = [(z + 8 - dz) % 8 for dz in pair]
+
+        def assemble(dx, _):
+            first = ((x + 4 - dx) % 4) * 32
+            for h, pz in enumerate(places):
+                for q in range(2):
+                    left0 = unpack(left_in, first + 16 * q + pz, False)
+                    left1 = unpack(left_in, first + 16 * q + 8 + pz, False)
+                    columns = pl.ds(pl.multiple_of(256 * dx + 128 * q, 128), 128)
+                    a_ref[48 * h : 48 * h + 48, columns] = jnp.concatenate(left0 + left1, axis=0).astype(BF16)
+            return 0
+
+        lax.fori_loop(0, 4, assemble, 0)
+
+        def step(px, _):
+            product = dot(a_ref[...], b_ref[pl.ds(2 * px, 2)].reshape(256, 1024), 1, 1)
+            for h, pz in enumerate(places):
+                for q in range(2):
+                    for g in range(2):
+                        block = product[48 * h + 24 * g : 48 * h + 24 * g + 24, 128 * q : 128 * q + 128]
+                        back_ref[px * 32 + 16 * q + 8 * g + pz] = pack(block)
+            return 0
+
+        lax.fori_loop(0, 4, step, 0)
+        send_pair(back_ref, home_ref, s_back, s_home.at[at], pair, -1)
+
+    for at, pair in enumerate(PAIRS):
+        multiply(at, pair)
     home_ref[me] = back_ref[me]
     others = pl.ds(0, CHIPS - 1)
-    pltpu.make_async_copy(send_ref.at[others, used], send_ref.at[others, used], s_send).wait()
+    pltpu.make_async_copy(left_out.at[others, used], left_out.at[others, used], s_left_out).wait()
+    pltpu.make_async_copy(right_out.at[others, used], right_out.at[others, used], s_right_out).wait()
 
     def widen(c, _):
         sums_ref[pl.ds(pl.multiple_of(c * ROWS, 8), ROWS), :] = home_ref[c].astype(F32)[0:ROWS]
         return 0
 
-    for q in range(4):
-        arrived = home_ref.at[pl.ds(0, 31 if q == 0 else 32), sent]
-        pltpu.make_async_copy(arrived, arrived, s_home.at[q]).wait()
-        first = ((x + 4 - q) % 4) * 32
-        lax.fori_loop(0, 32, lambda c, _, first=first: widen(first + c, _), 0, unroll=4)
+    for at, pair in enumerate(PAIRS):
+        arrived = home_ref.at[pl.ds(0, 31 if pair[0] == 0 else 32), used]
+        pltpu.make_async_copy(arrived, arrived, s_home.at[at]).wait()
+        for dz in pair:
+            pz = (z + dz) % 8
+            lax.fori_loop(0, 16, lambda r, _, pz=pz: widen(8 * r + pz, _), 0, unroll=4)
 
     lanes = lax.broadcasted_iota(jnp.int32, (CHIPS, 128), 1)
 
@@ -349,7 +352,7 @@
         return 0
 
     lax.fori_loop(0, 2, finish_four, 0)
-    pltpu.make_async_copy(back_ref.at[others, sent], back_ref.at[others, sent], s_back).wait()
+    pltpu.make_async_copy(back_ref.at[others, used], back_ref.at[others, used], s_back).wait()
 
 
 def shards(pair, tile_mask, chain_ids, in_gain, in_bias, w_ab, w_gate, out_gain, out_bias, w_out):
@@ -369,15 +372,16 @@
             pltpu.VMEM((TILES, 128, C), BF16),
             pltpu.VMEM((TILES, 128), F32),
             pltpu.VMEM((512, C), BF16),
-            pltpu.VMEM((32 * SLOT, 128), F32),
+            pltpu.VMEM((32 * STAGE, 128), F32),
+            pltpu.VMEM((CHIPS, SLOT, 128), BF16),
+            pltpu.VMEM((CHIPS, SLOT, 128), BF16),
             pltpu.VMEM((CHIPS, SLOT, 128), BF16),
             pltpu.VMEM((CHIPS, SLOT, 128), BF16),
             pltpu.VMEM((ROWS, COLS, C), F32),
-            pltpu.VMEM((4, 384, 256), BF16),
-            pltpu.VMEM((4, 8, 128, 256), BF16),
-            pltpu.VMEM((4, 384, 256), F32),
-            pltpu.VMEM((CHIPS, HOME, 128), BF16),
-            pltpu.VMEM((CHIPS, HOME, 128), BF16),
+            pltpu.VMEM((96, 1024), BF16),
+            pltpu.VMEM((8, 128, 1024), BF16),
+            pltpu.VMEM((CHIPS, SLOT, 128), BF16),
+            pltpu.VMEM((CHIPS, SLOT, 128), BF16),
             pltpu.VMEM((CHIPS * ROWS, 128), F32),
             pltpu.VMEM((C, 128), F32),
             pltpu.VMEM((C, 128), F32),
@@ -385,6 +389,8 @@
             pltpu.SemaphoreType.REGULAR,
             pltpu.SemaphoreType.REGULAR,
             pltpu.SemaphoreType.DMA(()),
+            pltpu.SemaphoreType.DMA(()),
+            pltpu.SemaphoreType.DMA((4,)),
             pltpu.SemaphoreType.DMA((4,)),
             pltpu.SemaphoreType.DMA((4,)),
             pltpu.SemaphoreType.DMA((4,)),

time: 63.9 us -> 56 us (0.88)
  Pallas kernels: 63 us -> 55.1 us
    pallas_call x1, Pallas kernels: 63 us -> 55.1 us  [shards(): pl.pallas_call(kernel, out_shape=pltpu.VMEM((ROWS, COLS, C), BF16), in_sp...]
where the time goes in v5:
time: 56 us; the launch traced here: 55.9 us
  Pallas kernels  55.1 us (98%)
  local copies, waits for them, and re-layouts  0.82 us (1%)
    pallas_call x1, Pallas kernels, shards(): pl.pallas_call(kernel, out_shape=pltpu.VMEM((ROWS, COLS, C), BF16), in_sp...  55.1 us

profile of v5, /device:TPU:1, one launch (start us, length us, event | category | flops | bytes accessed | tf_op | source)
XLA Modules:
  0.0 55.9 jit_solution(11021456540749766388)
XLA Ops:
  0.0 55.1 %shard_map.100 = bf16[24,96,128]{2,1,0:T(8,128)(2,1)S(1)} custom-call(bf16[24,96,128]{2,1,0:T(8,128)(2,1)} %pair_hbm.1, s32[6,6]{1,0:T(8,128)} %tile_hbm.1, s32[6,128]{1,0:T(8,128)} %bitcast.5, f32[1,128]{1,0:T(1,128)} %bitcast.6, f32[1,128]{1,0:T(1,128)} %bitcast.7, bf16[128,512]{1,0:T(8,128)(2,1)} %w_ab_hbm.1, bf16[128,128]{1,0:T(8,128)(2,1)} %w_gate_hbm.1, ...), custom_call_target="tpu_custom_call" | custom-call | tf_op jit(solution)/shard_map/pallas_call | solution.py:364
  55.1 0.8 %copy.12 = bf16[24,96,128]{2,1,0:T(8,128)(2,1)} copy(bf16[24,96,128]{2,1,0:T(8,128)(2,1)S(1)} %shard_map.100) | data formatting | bytes 1179648

commit v6 on v5

--- a/solution.py
+++ b/solution.py
@@ -317,7 +317,7 @@
         pltpu.make_async_copy(arrived, arrived, s_home.at[at]).wait()
         for dz in pair:
             pz = (z + dz) % 8
-            lax.fori_loop(0, 16, lambda r, _, pz=pz: widen(8 * r + pz, _), 0, unroll=4)
+            lax.fori_loop(0, 16, lambda r, _, pz=pz: widen(8 * r + pz, _), 0, unroll=16)
 
     lanes = lax.broadcasted_iota(jnp.int32, (CHIPS, 128), 1)
 
@@ -344,14 +344,14 @@
         natural = jnp.concatenate([projected[0:24], projected[48:72], projected[24:48], projected[72:96]], axis=0)
         out_ref[i] = (gate_ref[i] * natural).astype(BF16)
 
-    lax.fori_loop(0, 16, finish_main, 0, unroll=4)
+    lax.fori_loop(0, 16, finish_main, 0, unroll=8)
 
     def finish_four(h, _):
         for q in range(4):
             finish_rest(4 * h + q, q)
         return 0
 
-    lax.fori_loop(0, 2, finish_four, 0)
+    lax.fori_loop(0, 2, finish_four, 0, unroll=2)
     pltpu.make_async_copy(back_ref.at[others, used], back_ref.at[others, used], s_back).wait()
 
 

time: 56 us -> 55.3 us (0.987)
  Pallas kernels: 55.1 us -> 54.4 us
    pallas_call x1, Pallas kernels: 55.1 us -> 54.4 us  [shards(): pl.pallas_call(kernel, out_shape=pltpu.VMEM((ROWS, COLS, C), BF16), in_sp...]
where the time goes in v6:
time: 55.3 us; the launch traced here: 55.2 us
  Pallas kernels  54.4 us (98%)
  local copies, waits for them, and re-layouts  0.82 us (1%)
    pallas_call x1, Pallas kernels, shards(): pl.pallas_call(kernel, out_shape=pltpu.VMEM((ROWS, COLS, C), BF16), in_sp...  54.4 us

profile of v6, /device:TPU:1, one launch (start us, length us, event | category | flops | bytes accessed | tf_op | source)
XLA Modules:
  0.0 55.2 jit_solution(10880952405415316444)
XLA Ops:
  0.0 54.4 %shard_map.100 = bf16[24,96,128]{2,1,0:T(8,128)(2,1)S(1)} custom-call(bf16[24,96,128]{2,1,0:T(8,128)(2,1)} %pair_hbm.1, s32[6,6]{1,0:T(8,128)} %tile_hbm.1, s32[6,128]{1,0:T(8,128)} %bitcast.5, f32[1,128]{1,0:T(1,128)} %bitcast.6, f32[1,128]{1,0:T(1,128)} %bitcast.7, bf16[128,512]{1,0:T(8,128)(2,1)} %w_ab_hbm.1, bf16[128,128]{1,0:T(8,128)(2,1)} %w_gate_hbm.1, ...), custom_call_target="tpu_custom_call" | custom-call | tf_op jit(solution)/shard_map/pallas_call | solution.py:364
  54.4 0.8 %copy.12 = bf16[24,96,128]{2,1,0:T(8,128)(2,1)} copy(bf16[24,96,128]{2,1,0:T(8,128)(2,1)S(1)} %shard_map.100) | data formatting | bytes 1179648

commit v7 on v6

--- a/solution.py
+++ b/solution.py
@@ -372,7 +372,7 @@
             pltpu.VMEM((TILES, 128, C), BF16),
             pltpu.VMEM((TILES, 128), F32),
             pltpu.VMEM((512, C), BF16),
-            pltpu.VMEM((32 * STAGE, 128), F32),
+            pltpu.VMEM((33 * STAGE, 128), F32),
             pltpu.VMEM((CHIPS, SLOT, 128), BF16),
             pltpu.VMEM((CHIPS, SLOT, 128), BF16),
             pltpu.VMEM((CHIPS, SLOT, 128), BF16),
@@ -382,7 +382,7 @@
             pltpu.VMEM((8, 128, 1024), BF16),
             pltpu.VMEM((CHIPS, SLOT, 128), BF16),
             pltpu.VMEM((CHIPS, SLOT, 128), BF16),
-            pltpu.VMEM((CHIPS * ROWS, 128), F32),
+            pltpu.VMEM(((CHIPS + 1) * ROWS, 128), F32),
             pltpu.VMEM((C, 128), F32),
             pltpu.VMEM((C, 128), F32),
             pltpu.SemaphoreType.DMA((len(args),)),

time: 55.3 us -> 55.4 us (level)
  no operation moved by 1% of the time
where the time goes in v7:
time: 55.4 us; the launch traced here: 55.3 us
  Pallas kernels  54.4 us (98%)
  local copies, waits for them, and re-layouts  0.82 us (1%)
    pallas_call x1, Pallas kernels, shards(): pl.pallas_call(kernel, out_shape=pltpu.VMEM((ROWS, COLS, C), BF16), in_sp...  54.4 us

profile of v7, /device:TPU:1, one launch (start us, length us, event | category | flops | bytes accessed | tf_op | source)
XLA Modules:
  0.0 55.3 jit_solution(10693151456067225572)
XLA Ops:
  0.0 54.4 %shard_map.100 = bf16[24,96,128]{2,1,0:T(8,128)(2,1)S(1)} custom-call(bf16[24,96,128]{2,1,0:T(8,128)(2,1)} %pair_hbm.1, s32[6,6]{1,0:T(8,128)} %tile_hbm.1, s32[6,128]{1,0:T(8,128)} %bitcast.5, f32[1,128]{1,0:T(1,128)} %bitcast.6, f32[1,128]{1,0:T(1,128)} %bitcast.7, bf16[128,512]{1,0:T(8,128)(2,1)} %w_ab_hbm.1, bf16[128,128]{1,0:T(8,128)(2,1)} %w_gate_hbm.1, ...), custom_call_target="tpu_custom_call" | custom-call | tf_op jit(solution)/shard_map/pallas_call | solution.py:364
  54.4 0.8 %copy.12 = bf16[24,96,128]{2,1,0:T(8,128)(2,1)} copy(bf16[24,96,128]{2,1,0:T(8,128)(2,1)S(1)} %shard_map.100) | data formatting | bytes 1179648
